TPU v7x, 128 devices: a whole 4x4x4 slice. The times are simulated.
128 devices in a mesh: ctx: 8 (over x, core), dp: 16 (over y, z).
Axes of the slice: x: 4, y: 4, z: 4, core: 2. Of those that a mesh axis runs over, the one named last changes fastest.
Arguments:
- query: bfloat16 [16, 1024, 64, 192], P('dp', 'ctx'), may hold values from -48 to 48
- latent: bfloat16 [16, 1024, 576], P('dp', 'ctx'), may hold values from -6 to 6
- doc_lengths: int32 [16, 8], P('dp'), may hold values from 1 to 256, 1024 in all within a row
- w_kv: bfloat16 [16384, 512], replicated, may hold values from -0.25 to 0.25
- grad_out: bfloat16 [16, 1024, 64, 128], P('dp', 'ctx'), may hold values from -6 to 6
Outputs:
- d_query: bfloat16 [16, 1024, 64, 192], P('dp', 'ctx')
- d_latent: bfloat16 [16, 1024, 576], P('dp', 'ctx')
- d_w_kv: float32 [16384, 512], P(('ctx', 'dp'))
Inputs may be any that keep to these rules, and one draw needn't show every extreme that they name: `doc_lengths`: each row of 8 lengths sums to 1024; the longest document of every row has exactly 256 positions.
All inputs are finite; a program needn't handle non-finite values.
Results may differ from a plain program's by a relative error of at most 0.022.
Values may be sent and summed in bfloat16 or wider, within the bound.
No kernel may reach another device: no remote copies, remote signals or barrier semaphores. Data moves between devices by JAX's collectives and lax.ppermute only.
A program may use at most 256 MiB of HBM per device.

v0:
```python
import functools
import math

import jax
import jax.numpy as jnp
from jax import lax
from jax.experimental import pallas as pl
from jax.experimental.pallas import tpu as pltpu
from jax.sharding import Mesh
from jax.sharding import PartitionSpec as P

F32 = jnp.float32
BF16 = jnp.bfloat16
NX, NCORE, NY, NZ = 4, 2, 4, 4
HEADS = 64
NOPE = 128
ROPE = 64
WIDTH = NOPE + ROPE
VDIM = 128
HCOLS = NOPE + VDIM
LAT = 512
ROWS = 128
CHIP = NCORE * ROWS
KEYS = 2 * CHIP
GROUP = 8
PER_STEP = 4
SCALE = 1.0 / math.sqrt(WIDTH)
LOG2E = math.log2(math.e)
NT = (((1,), (1,)), ((), ()))
TN = (((0,), (0,)), ((), ()))


def mm(a, b, dims=(((1,), (0,)), ((), ()))):
    return lax.dot_general(a, b, dims, preferred_element_type=F32)


def main_kernel(leading, *refs):
    info, q_own, q_got, g_own, g_got, w_ref, lat_ref, latt_ref, rope_ref, low_ref = refs[:10]
    dq_ref, send_ref, dw_ref, dlat_ref, drope_ref, bias_ref = refs[-6:]
    first_core = info[0] == 0

    @pl.when(pl.program_id(0) == 0)
    def _():
        key = lax.broadcasted_iota(jnp.int32, (KEYS, CHIP), 0)
        row = lax.broadcasted_iota(jnp.int32, (KEYS, CHIP), 1)
        ok = (key >= low_ref[...]) & (key <= row + CHIP)
        bias_ref[...] = jnp.where(ok, 0.0, -1e30)
        if leading:
            dlat_ref[...] = jnp.zeros_like(dlat_ref)
            drope_ref[...] = jnp.zeros_like(drope_ref)
        else:
            dlat_ref[...] = refs[10][...]
            drope_ref[...] = refs[11][...]

    rope = rope_ref[...]
    kv_all = mm(lat_ref[...], w_ref[...], NT).astype(BF16)
    dkvs, dropes = [], []
    for i in range(PER_STEP):
        qo, qr, go, gr = q_own[i], q_got[i], g_own[i], g_got[i]
        q = jnp.concatenate([jnp.where(first_core, qo, qr), jnp.where(first_core, qr, qo)], axis=1)
        g = jnp.concatenate([jnp.where(first_core, go, gr), jnp.where(first_core, gr, go)], axis=0)
        col = i * HCOLS
        k = jnp.concatenate([kv_all[:, col : col + NOPE], rope], axis=1)
        v = kv_all[:, col + NOPE : col + HCOLS]
        s = mm(k, q) * (SCALE * LOG2E) + bias_ref[...]
        e = jnp.exp2(s - jnp.max(s, axis=0, keepdims=True))
        r = 1.0 / jnp.sum(e, axis=0, keepdims=True)
        dp = mm(v, g, NT)
        delta = jnp.sum(e * dp, axis=0, keepdims=True) * r
        rs = r * SCALE
        ds = (e * (dp * rs - delta * rs)).astype(BF16)
        dq = mm(k, ds, TN).astype(BF16)
        dq_ref[i] = jnp.where(first_core, dq[:, :ROWS], dq[:, ROWS:])
        send_ref[i] = jnp.where(first_core, dq[:, ROWS:], dq[:, :ROWS])
        dk = mm(ds, q, NT)
        dv = mm((e * r).astype(BF16), g)
        dropes.append(dk[:, NOPE:])
        dkvs.append(jnp.concatenate([dk[:, :NOPE], dv], axis=1).astype(BF16))
    drope_ref[...] += functools.reduce(jnp.add, dropes)
    dkv = jnp.concatenate(dkvs, axis=1)
    dw = mm(latt_ref[...], dkv).astype(BF16)
    for j in range(2 * PER_STEP):
        part = dw[:, j * 128 : (j + 1) * 128]
        dw_ref[j // NZ, j % NZ] = part
    dlat_ref[...] += mm(dkv, w_ref[...])


def main_group(info, q_full, q_got, g_full, g_got, w_kv, lat, latt, rope, low, state):
    steps = GROUP // PER_STEP
    half = lambda i, info: (info[1] * steps + i, 0, 0)
    full = lambda i, info: ((2 * info[1] + info[0]) * steps + i, 0, 0)
    whole = lambda i, info: (0, 0)
    w_rows = lambda i, info: ((2 * info[1] + info[0]) * steps + i, 0)
    ys = 2 * PER_STEP // NZ
    in_specs = [
        pl.BlockSpec((PER_STEP, WIDTH, ROWS), full),
        pl.BlockSpec((PER_STEP, WIDTH, ROWS), half),
        pl.BlockSpec((PER_STEP, ROWS, VDIM), full),
        pl.BlockSpec((PER_STEP, ROWS, VDIM), half),
        pl.BlockSpec((PER_STEP * HCOLS, LAT), w_rows),
        pl.BlockSpec((KEYS, LAT), whole),
        pl.BlockSpec((LAT, KEYS), whole),
        pl.BlockSpec((KEYS, ROPE), whole),
        pl.BlockSpec((1, CHIP), whole),
    ]
    aliases = {}
    if state:
        in_specs += [
            pl.BlockSpec((KEYS, LAT), whole),
            pl.BlockSpec((KEYS, ROPE), whole),
            pl.BlockSpec(memory_space=pl.ANY),
            pl.BlockSpec(memory_space=pl.ANY),
        ]
        aliases = {12: 0, 13: 1}
    grid_spec = pltpu.PrefetchScalarGridSpec(
        num_scalar_prefetch=1,
        grid=(steps,),
        in_specs=in_specs,
        out_specs=[
            pl.BlockSpec((PER_STEP, WIDTH, ROWS), full),
            pl.BlockSpec((PER_STEP, WIDTH, ROWS), half),
            pl.BlockSpec((ys, NZ, LAT, 128), lambda i, info: (i, 0, 0, 0)),
            pl.BlockSpec((KEYS, LAT), whole),
            pl.BlockSpec((KEYS, ROPE), whole),
        ],
        scratch_shapes=[pltpu.VMEM((KEYS, CHIP), F32)],
    )
    flops = 2 * GROUP * KEYS * CHIP
    return pl.pallas_call(
        functools.partial(main_kernel, not state),
        grid_spec=grid_spec,
        out_shape=[
            pltpu.HBM((HEADS, WIDTH, ROWS), BF16),
            pltpu.HBM((HEADS // 2, WIDTH, ROWS), BF16),
            pltpu.HBM((4, 4, LAT, 128), BF16),
            pltpu.HBM((KEYS, LAT), F32),
            pltpu.HBM((KEYS, ROPE), F32),
        ],
        input_output_aliases=aliases,
        compiler_params=pltpu.CompilerParams(
            dimension_semantics=("arbitrary",), vmem_limit_bytes=48 * 1024 * 1024
        ),
        cost_estimate=pl.CostEstimate(
            flops=flops, bytes_accessed=10 * 1024 * 1024, transcendentals=0
        ),
        name="main_group",
    )(info, q_full, q_got, g_full, g_got, w_kv, lat, latt, rope, low, *state)


def window_kernel(info, own, mate, prev_same, prev_mate, lat_ref, latt_ref, rope_ref):
    first_core = info[0] == 0

    def pair(mine, other):
        return [jnp.where(first_core, mine, other), jnp.where(first_core, other, mine)]

    window = jnp.concatenate(
        pair(prev_same[...], prev_mate[...]) + pair(own[...], mate[...]), axis=1
    )
    latt_ref[...] = window[:LAT]
    lat_ref[...] = window[:LAT].T
    rope_ref[...] = window[LAT:].T


def window_of(info, pieces):
    return pl.pallas_call(
        window_kernel,
        in_specs=[pl.BlockSpec(memory_space=pltpu.SMEM)]
        + [pl.BlockSpec(memory_space=pltpu.VMEM)] * 4,
        out_shape=[
            jax.ShapeDtypeStruct((KEYS, LAT), BF16),
            jax.ShapeDtypeStruct((LAT, KEYS), BF16),
            jax.ShapeDtypeStruct((KEYS, ROPE), BF16),
        ],
        compiler_params=pltpu.CompilerParams(vmem_limit_bytes=32 * 1024 * 1024),
        name="window",
    )(info, *pieces)


def place_kernel(info, got_ref, held_ref, out_ref):
    out_ref[...] = got_ref[...]


def place(info, got, held):
    block = (GROUP, WIDTH, ROWS)
    grid_spec = pltpu.PrefetchScalarGridSpec(
        num_scalar_prefetch=1,
        grid=(NX,),
        in_specs=[
            pl.BlockSpec(block, lambda i, info: (i, 0, 0)),
            pl.BlockSpec(memory_space=pl.ANY),
        ],
        out_specs=pl.BlockSpec(block, lambda i, info: (2 * i + 1 - info[0], 0, 0)),
    )
    return pl.pallas_call(
        place_kernel,
        grid_spec=grid_spec,
        out_shape=pltpu.HBM((HEADS, WIDTH, ROWS), BF16),
        input_output_aliases={2: 0},
        compiler_params=pltpu.CompilerParams(dimension_semantics=("arbitrary",)),
        cost_estimate=pl.CostEstimate(flops=0, bytes_accessed=4 * 1024 * 1024, transcendentals=0),
        name="place",
    )(info, got, held)


def start_of(lengths, positions):
    ends = jnp.cumsum(lengths)
    picked = jnp.where(ends[None, :] <= positions[:, None], lengths[None, :], 0)
    return jnp.sum(picked, axis=1)


def ring(distance):
    return [(i, (i + distance) % 4) for i in range(4)]


def pick(blocks, index):
    return lax.dynamic_index_in_dim(blocks, index, 0, keepdims=False)


def exchange(blocks, axis, me):
    got = [pick(blocks, me)]
    for distance in (1, 3, 2):
        sent = pick(blocks, lax.rem(me + distance, 4))
        got.append(lax.ppermute(sent, axis, ring(distance)))
    return got


def total(parts):
    return functools.reduce(jnp.add, [part.astype(F32) for part in parts])


def all_to_all(blocks, axis):
    return lax.all_to_all(blocks, axis, 0, 0, tiled=True)


def summed(parts):
    return jnp.sum(parts.astype(F32), axis=0).astype(BF16)


def per_device(query, latent, doc_lengths, w_kv, grad_out):
    x, core = lax.axis_index("x"), lax.axis_index("core")
    y, z = lax.axis_index("y"), lax.axis_index("z")
    swap = [(0, 1), (1, 0)]
    both = ("x", "core")
    tie = lax.optimization_barrier

    def other_half(full):
        parts = full.reshape(NX, NCORE, GROUP, full.shape[1], full.shape[2])
        chosen = lax.dynamic_index_in_dim(parts, 1 - core, 1, keepdims=False)
        return chosen.reshape(HEADS // 2, full.shape[1], full.shape[2])

    own = latent[0].T
    mate = lax.ppermute(own, "core", swap)
    prev_same = lax.ppermute(own, both, [(2 * i + c, 2 * i + 2 + c) for i in range(3) for c in range(2)])
    prev_mate = lax.ppermute(
        own, both, [(2 * i + c, 2 * i + 2 + 1 - c) for i in range(3) for c in range(2)]
    )
    q_full = query[0].transpose(1, 2, 0)
    q_got = lax.ppermute(other_half(q_full), "core", swap)
    g_full = tie(grad_out[0].transpose(1, 0, 2))
    g_got = lax.ppermute(other_half(g_full), "core", swap)

    core_info = core.astype(jnp.int32).reshape(1)
    lat, latt, rope = window_of(core_info, (own, mate, prev_same, prev_mate))
    base = x * CHIP
    starts = start_of(doc_lengths[0], base + jnp.arange(CHIP, dtype=jnp.int32))
    low = (starts - (base - CHIP)).astype(jnp.int32).reshape(1, CHIP)

    def main(ahead, state):
        group = lax.rem(x + ahead, NX)
        info = jnp.stack([core, group]).astype(jnp.int32)
        dq, send, dw, dlat, drope = main_group(
            info, q_full, q_got, g_full, g_got, w_kv, lat, latt, rope, low, state
        )
        return dw, (dlat, drope, dq, send)

    dw, state = main(1, ())
    from_left = lax.ppermute(dw, "x", ring(1))
    dw, state = main(3, state)
    from_right = lax.ppermute(dw, "x", ring(3))
    dw, state = main(2, state)
    across = all_to_all(dw, "y")
    dw, state = main(0, state)
    dlat, drope, dq, send = state

    across = summed(across)
    mine = total([dw, from_left, from_right]).astype(BF16)
    part_a = all_to_all(mine[:, :, : LAT // 2], "y")
    rows_b = NY * LAT // 2
    part_b = jnp.swapaxes(mine[:, :, LAT // 2 :], 0, 1).reshape(NZ, rows_b, 128)
    part_b = total(exchange(jnp.concatenate([part_b, across], axis=1), "z", z))
    across = lax.ppermute(part_b[rows_b:].astype(BF16), "x", ring(2))
    part_b = part_b[:rows_b].astype(BF16).reshape(NY, LAT // 2, 128)
    part_b = all_to_all(part_b, "y")
    part_a = total(exchange(summed(part_a), "z", z))
    part_b = jnp.sum(part_b.astype(F32), axis=0)
    d_weight = (jnp.concatenate([part_a, part_b], axis=0) + across.astype(F32)).T

    terms = jnp.concatenate([dlat, drope], axis=-1)
    blocks = terms.reshape(4, ROWS, LAT + ROPE)
    mine = pick(blocks, 2 + core)
    from_mate = lax.ppermute(pick(blocks, 3 - core).astype(BF16), "core", swap)
    from_next = lax.ppermute(
        pick(blocks, core).astype(BF16),
        both,
        [(2 * i + 2 + c, 2 * i + c) for i in range(3) for c in range(2)],
    )
    from_next_mate = lax.ppermute(
        pick(blocks, 1 - core).astype(BF16),
        both,
        [(2 * i + 2 + c, 2 * i + 1 - c) for i in range(3) for c in range(2)],
    )
    d_latent = total([mine, from_mate, from_next, from_next_mate]).astype(BF16)

    got = lax.ppermute(send, "core", swap)
    d_query = place(core_info, got, dq)
    return (d_query.transpose(2, 0, 1)[None], d_latent[None], d_weight)


def solution(mesh):
    fine = Mesh(mesh.devices.reshape(NX, NCORE, NY, NZ), ("x", "core", "y", "z"))
    dp, ctx = ("y", "z"), ("x", "core")
    in_specs = (P(dp, ctx, None, None), P(dp, ctx, None), P(dp, None), P(), P(dp, ctx, None, None))
    out_specs = (P(dp, ctx, None, None), P(dp, ctx, None), P(("x", "core", "y", "z"), None))
    return jax.shard_map(
        per_device, mesh=fine, in_specs=in_specs, out_specs=out_specs, check_vma=False
    )
```

profile of v0, /device:TPU:8, one launch (start us, length us, event | category | flops | bytes accessed | tf_op | source)
XLA Modules:
  0.0 150.0 jit_solution(1394937102724187172)
XLA Ops:
  0.6 2.8 %constant_dynamic-slice_fusion.5 = bf16[4,1,8,192,128]{4,3,2,1,0:T(8,128)(2,1)} fusion(bf16[4,2,8,192,128]{4,3,2,1,0:T(8,128)(2,1)} %bitcast.93, s32[]{:T(128)S(6)} %select_n.41), kind=kLoop, calls=%fused_computation.47 | loop fusion | bytes 3145732 | tf_op jit(solution)/shard_map/jit(dynamic_index_in_dim)/dynamic_slice | solution.py:248
  3.5 1.4 copy.46
  4.9 1.1 constant_dynamic-slice_fusion.4
  6.4 4.0 %collective-permute-start.3 = (bf16[576,128]{1,0:T(8,128)(2,1)S(1)}, bf16[576,128]{1,0:T(8,128)(2,1)}, u32[]{:S(2)}, u32[]{:S(2)}) collective-permute-start(bf16[576,128]{1,0:T(8,128)(2,1)S(1)} %bitcast.86), channel_id=1, source_target_pairs={{0,32},{16,48},{32,64},{48,80},{64,96},{80,112},{1,33},{17,49},{33... | collective-permute-start | bytes 442376 | tf_op jit(solution)/shard_map/ppermute | solution.py:253
  10.5 3.3 %collective-permute-start.4 = (bf16[576,128]{1,0:T(8,128)(2,1)S(1)}, bf16[576,128]{1,0:T(8,128)(2,1)}, u32[]{:S(2)}, u32[]{:S(2)}) collective-permute-start(bf16[576,128]{1,0:T(8,128)(2,1)S(1)} %bitcast.87), channel_id=1, source_target_pairs={{0,48},{16,32},{32,80},{48,64},{64,112},{80,96},{1,49},{17,33},{33... | collective-permute-start | bytes 442376 | tf_op jit(solution)/shard_map/ppermute | solution.py:254
  14.1 2.8 %collective-permute-done.4.prev_mate = bf16[576,128]{1,0:T(8,128)(2,1)} collective-permute-done((bf16[576,128]{1,0:T(8,128)(2,1)S(1)}, bf16[576,128]{1,0:T(8,128)(2,1)}, u32[]{:S(2)}, u32[]{:S(2)}) %collective-permute-start.4) | collective-permute-done | bytes 147488 | tf_op jit(solution)/shard_map/ppermute | solution.py:254
  16.9 1.3 window.1
  18.2 12.2 %main_group.4 = (bf16[64,192,128]{2,1,0:T(8,128)(2,1)}, bf16[32,192,128]{2,1,0:T(8,128)(2,1)}, bf16[4,4,512,128]{3,2,1,0:T(8,128)(2,1)}, f32[512,512]{1,0:T(8,128)}, f32[512,64]{1,0:T(8,128)}) custom-call(s32[2]{0:T(128)S(1)} %get-tuple-element.69.refs_0_, bf16[64,192,128]{2,1,0:T(8,128)(2,1)} %bitcast.94, ...), custom_call_target="tpu_custom_call" | custom-call | flops 2097152 | bytes 10485760 | tf_op jit(solution)/shard_map/main_group/pallas_call | solution.py:129
  30.4 1.2 copy-done.9
  31.6 0.9 copy-done.12
  32.6 12.2 %main_group.5 = (bf16[64,192,128]{2,1,0:T(8,128)(2,1)}, bf16[32,192,128]{2,1,0:T(8,128)(2,1)}, bf16[4,4,512,128]{3,2,1,0:T(8,128)(2,1)}, f32[512,512]{1,0:T(8,128)}, f32[512,64]{1,0:T(8,128)}) custom-call(s32[2]{0:T(128)S(1)} %get-tuple-element.68.refs_0_, bf16[64,192,128]{2,1,0:T(8,128)(2,1)} %bitcast.95, ...), custom_call_target="tpu_custom_call", output_to_operand_aliasing={{0}: (12, {}), {1}: (13, {})} | custom-call | flops 2097152 | bytes 10485760 | tf_op jit(solution)/shard_map/main_group/pallas_call | solution.py:129
  44.7 3.4 %collective-permute-start.10 = (bf16[4,4,512,128]{3,2,1,0:T(8,128)(2,1)}, bf16[4,4,512,128]{3,2,1,0:T(8,128)(2,1)}, u32[]{:S(2)}, u32[]{:S(2)}) collective-permute-start(bf16[4,4,512,128]{3,2,1,0:T(8,128)(2,1)} %get-tuple-element.47), channel_id=1, source_target_pairs={{0,96},{32,0},{64,32},{96,64},{1,97},{33,1},{65,33},{97,65},{2,98}... | collective-permute-start | bytes 6291464 | tf_op jit(solution)/shard_map/ppermute | solution.py:279
  48.2 1.0 copy-done.2
  49.3 1.0 copy-done.5
  50.3 1.2 copy-done.8
  51.5 0.9 copy-done.11
  52.5 12.2 %main_group.6 = (bf16[64,192,128]{2,1,0:T(8,128)(2,1)}, bf16[32,192,128]{2,1,0:T(8,128)(2,1)}, bf16[4,4,512,128]{3,2,1,0:T(8,128)(2,1)}, f32[512,512]{1,0:T(8,128)}, f32[512,64]{1,0:T(8,128)}) custom-call(s32[2]{0:T(128)S(1)} %get-tuple-element.67.refs_0_, bf16[64,192,128]{2,1,0:T(8,128)(2,1)} %bitcast.96, ...), custom_call_target="tpu_custom_call", output_to_operand_aliasing={{0}: (12, {}), {1}: (13, {})} | custom-call | flops 2097152 | bytes 10485760 | tf_op jit(solution)/shard_map/main_group/pallas_call | solution.py:129
  64.7 5.0 %all-to-all-start.1 = ((bf16[4,4,512,128]{3,2,1,0:T(8,128)(2,1)}), bf16[4,4,512,128]{3,2,1,0:T(8,128)(2,1)}, u32[]{:S(2)}, u32[]{:S(2)}) async-start(bf16[4,4,512,128]{3,2,1,0:T(8,128)(2,1)} %get-tuple-element.48), calls=%async_computation.1 | async-start | bytes 4194304 | tf_op jit(solution)/shard_map/all_to_all | solution.py:232
  69.8 12.2 %main_group.7 = (bf16[64,192,128]{2,1,0:T(8,128)(2,1)}, bf16[32,192,128]{2,1,0:T(8,128)(2,1)}, bf16[4,4,512,128]{3,2,1,0:T(8,128)(2,1)}, f32[512,512]{1,0:T(8,128)}, f32[512,64]{1,0:T(8,128)}) custom-call(s32[2]{0:T(128)S(1)} %get-tuple-element.66.refs_0_, bf16[64,192,128]{2,1,0:T(8,128)(2,1)} %bitcast.97, ...), custom_call_target="tpu_custom_call", output_to_operand_aliasing={{0}: (12, {}), {1}: (13, {})} | custom-call | flops 2097152 | bytes 10485760 | tf_op jit(solution)/shard_map/main_group/pallas_call | solution.py:129
  82.0 13.1 %all-to-all-done.1 = bf16[4,4,512,128]{3,2,1,0:T(8,128)(2,1)} async-done(((bf16[4,4,512,128]{3,2,1,0:T(8,128)(2,1)}), bf16[4,4,512,128]{3,2,1,0:T(8,128)(2,1)}, u32[]{:S(2)}, u32[]{:S(2)}) %all-to-all-start.1) | async-done | bytes 2097184 | tf_op jit(solution)/shard_map/all_to_all | solution.py:232
  95.1 2.0 %reduce_sum.44 = bf16[4,512,128]{2,1,0:T(8,128)(2,1)S(1)} reduce(bf16[4,4,512,128]{3,2,1,0:T(8,128)(2,1)} %all-to-all-done.1, bf16[]{:T(256)} %constant.93.clone.1), dimensions={0}, to_apply=%region_3.4 | reduce | flops 786432 | bytes 2621442 | tf_op jit(solution)/shard_map/reduce_sum | solution.py:236
  97.1 3.1 %add_convert_fusion = bf16[4,4,512,128]{3,2,1,0:T(8,128)(2,1)S(1)} fusion(bf16[4,4,512,128]{3,2,1,0:T(8,128)(2,1)} %collective-permute-done.10, bf16[4,4,512,128]{3,2,1,0:T(8,128)(2,1)} %collective-permute-done.9, bf16[4,4,512,128]{3,2,1,0:T(8,128)(2,1)S(1)} %copy-done.16), kind=kLoop, calls=%fused_computation | loop fusion | flops 6291456 | bytes 8388608 | tf_op jit(solution)/shard_map/convert_element_type | solution.py:286
  100.2 1.1 fusion.18
  101.4 1.1 fusion.8
  102.5 1.9 %collective-permute-start.14 = (bf16[1536,128]{1,0:T(8,128)(2,1)}, bf16[1536,128]{1,0:T(8,128)(2,1)}, u32[]{:S(2)}, u32[]{:S(2)}) collective-permute-start(bf16[1536,128]{1,0:T(8,128)(2,1)} %get-tuple-element.57), channel_id=1, source_target_pairs={{0,1},{1,2},{2,3},{3,0},{4,5},{5,6},{6,7},{7,4},{8,9},{9,10},{10,1... | collective-permute-start | bytes 1179656 | tf_op jit(solution)/shard_map/ppermute | solution.py:223
  104.4 2.1 %collective-permute-start.15 = (bf16[1536,128]{1,0:T(8,128)(2,1)}, bf16[1536,128]{1,0:T(8,128)(2,1)}, u32[]{:S(2)}, u32[]{:S(2)}) collective-permute-start(bf16[1536,128]{1,0:T(8,128)(2,1)} %get-tuple-element.58), channel_id=1, source_target_pairs={{0,3},{1,0},{2,1},{3,2},{4,7},{5,4},{6,5},{7,6},{8,11},{9,8},{10,9... | collective-permute-start | bytes 1179656 | tf_op jit(solution)/shard_map/ppermute | solution.py:223
  106.5 1.9 %collective-permute-start.16 = (bf16[1536,128]{1,0:T(8,128)(2,1)}, bf16[1536,128]{1,0:T(8,128)(2,1)}, u32[]{:S(2)}, u32[]{:S(2)}) collective-permute-start(bf16[1536,128]{1,0:T(8,128)(2,1)} %get-tuple-element.59), channel_id=1, source_target_pairs={{0,2},{1,3},{2,0},{3,1},{4,6},{5,7},{6,4},{7,5},{8,10},{9,11},{10,... | collective-permute-start | bytes 1179656 | tf_op jit(solution)/shard_map/ppermute | solution.py:223
  108.4 4.9 %all-to-all-start = ((bf16[4,4,256,128]{3,2,1,0:T(8,128)(2,1)}), bf16[4,4,256,128]{3,2,1,0:T(8,128)(2,1)S(1)}, u32[]{:S(2)}, u32[]{:S(2)}) async-start(bf16[4,4,256,128]{3,2,1,0:T(8,128)(2,1)} %get-tuple-element.55), calls=%async_computation | async-start | bytes 2097152 | tf_op jit(solution)/shard_map/all_to_all | solution.py:232
  113.3 1.3 pad_maximum_fusion
  114.6 1.0 copy-done.14
  115.7 0.8 copy.42
  116.5 0.8 copy.43
  117.3 0.8 copy.44
  118.1 1.0 constant_dynamic-slice_fusion.3
  119.3 1.3 collective-permute-start.7
  120.6 2.4 %collective-permute-done.15 = bf16[1536,128]{1,0:T(8,128)(2,1)} collective-permute-done((bf16[1536,128]{1,0:T(8,128)(2,1)}, bf16[1536,128]{1,0:T(8,128)(2,1)}, u32[]{:S(2)}, u32[]{:S(2)}) %collective-permute-start.15) | collective-permute-done | bytes 393248 | tf_op jit(solution)/shard_map/ppermute | solution.py:223
  122.9 1.3 collective-permute-start.8
  124.8 1.4 fusion.2
  126.3 0.7 slice.20
  127.0 4.9 %all-to-all-start.2 = ((bf16[4,256,128]{2,1,0:T(8,128)(2,1)}), bf16[4,256,128]{2,1,0:T(8,128)(2,1)S(1)}, u32[]{:S(2)}, u32[]{:S(2)}) async-start(bf16[4,256,128]{2,1,0:T(8,128)(2,1)} %bitcast.39), calls=%async_computation.2 | async-start | bytes 524288 | tf_op jit(solution)/shard_map/all_to_all | solution.py:232
  131.9 1.7 %fusion.15 = bf16[1,128,576]{1,2,0:T(8,128)(2,1)} fusion(bf16[128,576]{0,1:T(8,128)(2,1)} %collective-permute-done.8, bf16[128,576]{0,1:T(8,128)(2,1)} %collective-permute-done.7, bf16[128,576]{0,1:T(8,128)(2,1)S(1)} %collective-permute-done.6, f32[1,128,576]{1,2,0:T(8,128)S(1)} %copy.34), kind=kLoop, calls=%fused_computation.31 | loop fusion | flops 516096 | bytes 884736 | tf_op jit(solution)/shard_map/broadcast_in_dim | solution.py:316
  133.6 3.6 %place.1 = bf16[64,192,128]{2,1,0:T(8,128)(2,1)} custom-call(s32[1]{0:T(128)} %bitcast.info, bf16[32,192,128]{2,1,0:T(8,128)(2,1)} %collective-permute-done.5.got_ref, bf16[64,192,128]{2,1,0:T(8,128)(2,1)} %get-tuple-element.42.held_ref), custom_call_target="tpu_custom_call", output_to_operand_aliasing={{}: (2, {})} | custom-call | bytes 4194304 | tf_op jit(solution)/shard_map/place/pallas_call | solution.py:194
  137.2 2.2 %collective-permute-start.17 = (bf16[512,128]{1,0:T(8,128)(2,1)S(1)}, bf16[512,128]{1,0:T(8,128)(2,1)S(1)}, u32[]{:S(2)}, u32[]{:S(2)}) collective-permute-start(bf16[512,128]{1,0:T(8,128)(2,1)S(1)} %slice.21), channel_id=1, source_target_pairs={{0,64},{32,96},{64,0},{96,32},{1,65},{33,97},{65,1},{97,33},{2,66}... | collective-permute-start | bytes 393224 | tf_op jit(solution)/shard_map/ppermute | solution.py:291
  139.7 1.8 %collective-permute-start.11 = (bf16[256,128]{1,0:T(8,128)(2,1)S(1)}, bf16[256,128]{1,0:T(8,128)(2,1)S(1)}, u32[]{:S(2)}, u32[]{:S(2)}) collective-permute-start(bf16[256,128]{1,0:T(8,128)(2,1)S(1)} %get-tuple-element.63), channel_id=1, source_target_pairs={{0,1},{1,2},{2,3},{3,0},{4,5},{5,6},{6,7},{7,4},{8,9},{9,10},{10,1... | collective-permute-start | bytes 196616 | tf_op jit(solution)/shard_map/ppermute | solution.py:223
  141.5 1.5 collective-permute-start.12
  143.0 3.0 %collective-permute-start.13 = (bf16[256,128]{1,0:T(8,128)(2,1)S(1)}, bf16[256,128]{1,0:T(8,128)(2,1)S(1)}, u32[]{:S(2)}, u32[]{:S(2)}) collective-permute-start(bf16[256,128]{1,0:T(8,128)(2,1)S(1)} %get-tuple-element.64), channel_id=1, source_target_pairs={{0,2},{1,3},{2,0},{3,1},{4,6},{5,7},{6,4},{7,5},{8,10},{9,11},{10,... | collective-permute-start | bytes 196616 | tf_op jit(solution)/shard_map/ppermute | solution.py:223
  146.6 2.5 %collective-permute-done.13 = bf16[256,128]{1,0:T(8,128)(2,1)S(1)} collective-permute-done((bf16[256,128]{1,0:T(8,128)(2,1)S(1)}, bf16[256,128]{1,0:T(8,128)(2,1)S(1)}, u32[]{:S(2)}, u32[]{:S(2)}) %collective-permute-start.13) | collective-permute-done | bytes 65568 | tf_op jit(solution)/shard_map/ppermute | solution.py:223
  149.1 0.8 copy.39
  (69 shorter events, 2.9 us)
Async XLA Ops:
  0.6 2.8 %copy-start.15 = (bf16[1,128,64,128]{3,2,1,0:T(8,128)(2,1)S(1)}, bf16[1,128,64,128]{3,2,1,0:T(8,128)(2,1)}, u32[]{:S(2)}) copy-start(bf16[1,128,64,128]{3,2,1,0:T(8,128)(2,1)} %param.9) | copy-start | bytes 6291460
  3.5 14.8 %collective-permute-start = (bf16[32,192,128]{2,1,0:T(8,128)(2,1)}, bf16[32,192,128]{2,1,0:T(8,128)(2,1)}, u32[]{:S(2)}, u32[]{:S(2)}) collective-permute-start(bf16[32,192,128]{2,1,0:T(8,128)(2,1)} %bitcast.6), channel_id=1, source_target_pairs={{0,16},{16,0},{1,17},{17,1},{2,18},{18,2},{3,19},{19,3},{4,20},{20... | collective-permute-start | bytes 4718600 | tf_op jit(solution)/shard_map/ppermute | solution.py:258
  4.8 25.6 %copy-start = (bf16[1,128,64,128]{3,1,2,0:T(8,128)(2,1)}, bf16[1,128,64,128]{3,1,2,0:T(8,128)(2,1)S(1)}, u32[]{:S(2)}) copy-start(bf16[1,128,64,128]{3,1,2,0:T(8,128)(2,1)S(1)} %copy.46) | copy-start | bytes 6291460
  4.8 1.6 %copy-start.13 = (bf16[1,128,576]{1,2,0:T(8,128)(2,1)S(1)}, bf16[1,128,576]{1,2,0:T(8,128)(2,1)}, u32[]{:S(2)}) copy-start(bf16[1,128,576]{1,2,0:T(8,128)(2,1)} %param.6) | copy-start | bytes 442372
  4.8 8.9 %copy-start.18 = (s32[1,8]{1,0:T(1,128)S(1)}, s32[1,8]{1,0:T(1,128)}, u32[]{:S(2)}) copy-start(s32[1,8]{1,0:T(1,128)} %param.7) | copy-start | bytes 100
  5.9 12.3 %collective-permute-start.1 = (bf16[32,128,128]{2,1,0:T(8,128)(2,1)}, bf16[32,128,128]{2,1,0:T(8,128)(2,1)S(1)}, u32[]{:S(2)}, u32[]{:S(2)}) collective-permute-start(bf16[32,128,128]{2,1,0:T(8,128)(2,1)} %bitcast.10), channel_id=1, source_target_pairs={{0,16},{16,0},{1,17},{17,1},{2,18},{18,2},{3,19},{19,3},{4,20},{20... | collective-permute-start | bytes 3145736 | tf_op jit(solution)/shard_map/ppermute | solution.py:260
  6.4 7.7 %collective-permute-start.2 = (bf16[576,128]{1,0:T(8,128)(2,1)S(1)}, bf16[576,128]{1,0:T(8,128)(2,1)}, u32[]{:S(2)}, u32[]{:S(2)}) collective-permute-start(bf16[576,128]{1,0:T(8,128)(2,1)S(1)} %bitcast.85), channel_id=1, source_target_pairs={{0,16},{16,0},{1,17},{17,1},{2,18},{18,2},{3,19},{19,3},{4,20},{20... | collective-permute-start | bytes 442376 | tf_op jit(solution)/shard_map/ppermute | solution.py:252
  6.4 7.7 %collective-permute-start.3 = (bf16[576,128]{1,0:T(8,128)(2,1)S(1)}, bf16[576,128]{1,0:T(8,128)(2,1)}, u32[]{:S(2)}, u32[]{:S(2)}) collective-permute-start(bf16[576,128]{1,0:T(8,128)(2,1)S(1)} %bitcast.86), channel_id=1, source_target_pairs={{0,32},{16,48},{32,64},{48,80},{64,96},{80,112},{1,33},{17,49},{33... | collective-permute-start | bytes 442376 | tf_op jit(solution)/shard_map/ppermute | solution.py:253
  10.5 6.4 %collective-permute-start.4 = (bf16[576,128]{1,0:T(8,128)(2,1)S(1)}, bf16[576,128]{1,0:T(8,128)(2,1)}, u32[]{:S(2)}, u32[]{:S(2)}) collective-permute-start(bf16[576,128]{1,0:T(8,128)(2,1)S(1)} %bitcast.87), channel_id=1, source_target_pairs={{0,48},{16,32},{32,80},{48,64},{64,112},{80,96},{1,49},{17,33},{33... | collective-permute-start | bytes 442376 | tf_op jit(solution)/shard_map/ppermute | solution.py:254
  18.2 12.2 %copy-start.1 = (bf16[512,512]{1,0:T(8,128)(2,1)}, bf16[512,512]{1,0:T(8,128)(2,1)S(1)}, u32[]{:S(2)}) copy-start(bf16[512,512]{1,0:T(8,128)(2,1)S(1)} %get-tuple-element.26.refs_6_) | copy-start | bytes 1572868
  18.2 12.2 %copy-start.4 = (bf16[512,512]{1,0:T(8,128)(2,1)}, bf16[512,512]{1,0:T(8,128)(2,1)S(1)}, u32[]{:S(2)}) copy-start(bf16[512,512]{1,0:T(8,128)(2,1)S(1)} %get-tuple-element.27.refs_7_) | copy-start | bytes 1572868
  30.4 1.2 copy-start.9
  31.6 0.9 copy-start.12
  44.7 52.4 %collective-permute-start.10 = (bf16[4,4,512,128]{3,2,1,0:T(8,128)(2,1)}, bf16[4,4,512,128]{3,2,1,0:T(8,128)(2,1)}, u32[]{:S(2)}, u32[]{:S(2)}) collective-permute-start(bf16[4,4,512,128]{3,2,1,0:T(8,128)(2,1)} %get-tuple-element.47), channel_id=1, source_target_pairs={{0,96},{32,0},{64,32},{96,64},{1,97},{33,1},{65,33},{97,65},{2,98}... | collective-permute-start | bytes 6291464 | tf_op jit(solution)/shard_map/ppermute | solution.py:279
  48.1 49.0 %collective-permute-start.9 = (bf16[4,4,512,128]{3,2,1,0:T(8,128)(2,1)}, bf16[4,4,512,128]{3,2,1,0:T(8,128)(2,1)}, u32[]{:S(2)}, u32[]{:S(2)}) collective-permute-start(bf16[4,4,512,128]{3,2,1,0:T(8,128)(2,1)} %get-tuple-element.46), channel_id=1, source_target_pairs={{0,32},{32,64},{64,96},{96,0},{1,33},{33,65},{65,97},{97,1},{2,34}... | collective-permute-start | bytes 6291464 | tf_op jit(solution)/shard_map/ppermute | solution.py:277
  48.2 1.0 copy-start.2
  49.3 1.0 copy-start.5
  50.3 1.2 copy-start.8
  51.5 0.9 copy-start.11
  64.7 5.1 %copy-start.3 = (bf16[512,512]{1,0:T(8,128)(2,1)S(1)}, bf16[512,512]{1,0:T(8,128)(2,1)}, u32[]{:S(2)}) copy-start(bf16[512,512]{1,0:T(8,128)(2,1)} %copy-done.1) | copy-start | bytes 1572868
  64.7 5.1 %copy-start.6 = (bf16[512,512]{1,0:T(8,128)(2,1)S(1)}, bf16[512,512]{1,0:T(8,128)(2,1)}, u32[]{:S(2)}) copy-start(bf16[512,512]{1,0:T(8,128)(2,1)} %copy-done.4) | copy-start | bytes 1572868
  64.7 5.1 %copy-start.7 = (f32[512,512]{1,0:T(8,128)S(1)}, f32[512,512]{1,0:T(8,128)}, u32[]{:S(2)}) copy-start(f32[512,512]{1,0:T(8,128)} %get-tuple-element.37.refs_10_) | copy-start | bytes 3145732
  64.7 5.1 %copy-start.10 = (f32[512,64]{1,0:T(8,128)S(1)}, f32[512,64]{1,0:T(8,128)}, u32[]{:S(2)}) copy-start(f32[512,64]{1,0:T(8,128)} %get-tuple-element.38.refs_11_) | copy-start | bytes 393220
  64.7 30.4 %all-to-all-start.1 = ((bf16[4,4,512,128]{3,2,1,0:T(8,128)(2,1)}), bf16[4,4,512,128]{3,2,1,0:T(8,128)(2,1)}, u32[]{:S(2)}, u32[]{:S(2)}) async-start(bf16[4,4,512,128]{3,2,1,0:T(8,128)(2,1)} %get-tuple-element.48), calls=%async_computation.1 | async-start | bytes 4194304 | tf_op jit(solution)/shard_map/all_to_all | solution.py:232
  81.9 15.2 %copy-start.16 = (bf16[4,4,512,128]{3,2,1,0:T(8,128)(2,1)S(1)}, bf16[4,4,512,128]{3,2,1,0:T(8,128)(2,1)}, u32[]{:S(2)}) copy-start(bf16[4,4,512,128]{3,2,1,0:T(8,128)(2,1)} %get-tuple-element.45) | copy-start | bytes 6291460
  81.9 51.6 %collective-permute-start.5 = (bf16[32,192,128]{2,1,0:T(8,128)(2,1)}, bf16[32,192,128]{2,1,0:T(8,128)(2,1)}, u32[]{:S(2)}, u32[]{:S(2)}) collective-permute-start(bf16[32,192,128]{2,1,0:T(8,128)(2,1)} %get-tuple-element.41), channel_id=1, source_target_pairs={{0,16},{16,0},{1,17},{17,1},{2,18},{18,2},{3,19},{19,3},{4,20},{20... | collective-permute-start | bytes 4718600 | tf_op jit(solution)/shard_map/ppermute | solution.py:314
  101.4 11.9 %copy-start.17 = (f32[512,64]{1,0:T(8,128)S(1)}, f32[512,64]{1,0:T(8,128)}, u32[]{:S(2)}) copy-start(f32[512,64]{1,0:T(8,128)} %get-tuple-element.44) | copy-start | bytes 393220
  102.5 16.8 %collective-permute-start.14 = (bf16[1536,128]{1,0:T(8,128)(2,1)}, bf16[1536,128]{1,0:T(8,128)(2,1)}, u32[]{:S(2)}, u32[]{:S(2)}) collective-permute-start(bf16[1536,128]{1,0:T(8,128)(2,1)} %get-tuple-element.57), channel_id=1, source_target_pairs={{0,1},{1,2},{2,3},{3,0},{4,5},{5,6},{6,7},{7,4},{8,9},{9,10},{10,1... | collective-permute-start | bytes 1179656 | tf_op jit(solution)/shard_map/ppermute | solution.py:223
  104.4 18.5 %collective-permute-start.15 = (bf16[1536,128]{1,0:T(8,128)(2,1)}, bf16[1536,128]{1,0:T(8,128)(2,1)}, u32[]{:S(2)}, u32[]{:S(2)}) collective-permute-start(bf16[1536,128]{1,0:T(8,128)(2,1)} %get-tuple-element.58), channel_id=1, source_target_pairs={{0,3},{1,0},{2,1},{3,2},{4,7},{5,4},{6,5},{7,6},{8,11},{9,8},{10,9... | collective-permute-start | bytes 1179656 | tf_op jit(solution)/shard_map/ppermute | solution.py:223
  106.5 18.3 %collective-permute-start.16 = (bf16[1536,128]{1,0:T(8,128)(2,1)}, bf16[1536,128]{1,0:T(8,128)(2,1)}, u32[]{:S(2)}, u32[]{:S(2)}) collective-permute-start(bf16[1536,128]{1,0:T(8,128)(2,1)} %get-tuple-element.59), channel_id=1, source_target_pairs={{0,2},{1,3},{2,0},{3,1},{4,6},{5,7},{6,4},{7,5},{8,10},{9,11},{10,... | collective-permute-start | bytes 1179656 | tf_op jit(solution)/shard_map/ppermute | solution.py:223
  108.4 18.6 %all-to-all-start = ((bf16[4,4,256,128]{3,2,1,0:T(8,128)(2,1)}), bf16[4,4,256,128]{3,2,1,0:T(8,128)(2,1)S(1)}, u32[]{:S(2)}, u32[]{:S(2)}) async-start(bf16[4,4,256,128]{3,2,1,0:T(8,128)(2,1)} %get-tuple-element.55), calls=%async_computation | async-start | bytes 2097152 | tf_op jit(solution)/shard_map/all_to_all | solution.py:232
  114.6 1.1 copy-start.14
  116.5 15.3 %collective-permute-start.6 = (bf16[128,576]{0,1:T(8,128)(2,1)}, bf16[128,576]{0,1:T(8,128)(2,1)S(1)}, u32[]{:S(2)}, u32[]{:S(2)}) collective-permute-start(bf16[128,576]{0,1:T(8,128)(2,1)} %bitcast.78), channel_id=1, source_target_pairs={{0,16},{16,0},{1,17},{17,1},{2,18},{18,2},{3,19},{19,3},{4,20},{20... | collective-permute-start | bytes 442376 | tf_op jit(solution)/shard_map/ppermute | solution.py:301
  119.3 12.6 %collective-permute-start.7 = (bf16[128,576]{0,1:T(8,128)(2,1)}, bf16[128,576]{0,1:T(8,128)(2,1)}, u32[]{:S(2)}, u32[]{:S(2)}) collective-permute-start(bf16[128,576]{0,1:T(8,128)(2,1)} %bitcast.104), channel_id=1, source_target_pairs={{32,0},{48,16},{64,32},{80,48},{96,64},{112,80},{33,1},{49,17},{65... | collective-permute-start | bytes 442376 | tf_op jit(solution)/shard_map/ppermute | solution.py:302
  122.9 8.9 %collective-permute-start.8 = (bf16[128,576]{0,1:T(8,128)(2,1)}, bf16[128,576]{0,1:T(8,128)(2,1)}, u32[]{:S(2)}, u32[]{:S(2)}) collective-permute-start(bf16[128,576]{0,1:T(8,128)(2,1)} %bitcast.103), channel_id=1, source_target_pairs={{32,16},{48,0},{64,48},{80,32},{96,80},{112,64},{33,17},{49,1},{65... | collective-permute-start | bytes 442376 | tf_op jit(solution)/shard_map/ppermute | solution.py:307
  127.0 19.0 %all-to-all-start.2 = ((bf16[4,256,128]{2,1,0:T(8,128)(2,1)}), bf16[4,256,128]{2,1,0:T(8,128)(2,1)S(1)}, u32[]{:S(2)}, u32[]{:S(2)}) async-start(bf16[4,256,128]{2,1,0:T(8,128)(2,1)} %bitcast.39), calls=%async_computation.2 | async-start | bytes 524288 | tf_op jit(solution)/shard_map/all_to_all | solution.py:232
  137.2 11.9 %collective-permute-start.17 = (bf16[512,128]{1,0:T(8,128)(2,1)S(1)}, bf16[512,128]{1,0:T(8,128)(2,1)S(1)}, u32[]{:S(2)}, u32[]{:S(2)}) collective-permute-start(bf16[512,128]{1,0:T(8,128)(2,1)S(1)} %slice.21), channel_id=1, source_target_pairs={{0,64},{32,96},{64,0},{96,32},{1,65},{33,97},{65,1},{97,33},{2,66}... | collective-permute-start | bytes 393224 | tf_op jit(solution)/shard_map/ppermute | solution.py:291
  139.7 6.4 %collective-permute-start.11 = (bf16[256,128]{1,0:T(8,128)(2,1)S(1)}, bf16[256,128]{1,0:T(8,128)(2,1)S(1)}, u32[]{:S(2)}, u32[]{:S(2)}) collective-permute-start(bf16[256,128]{1,0:T(8,128)(2,1)S(1)} %get-tuple-element.63), channel_id=1, source_target_pairs={{0,1},{1,2},{2,3},{3,0},{4,5},{5,6},{6,7},{7,4},{8,9},{9,10},{10,1... | collective-permute-start | bytes 196616 | tf_op jit(solution)/shard_map/ppermute | solution.py:223
  141.5 5.1 %collective-permute-start.12 = (bf16[256,128]{1,0:T(8,128)(2,1)S(1)}, bf16[256,128]{1,0:T(8,128)(2,1)S(1)}, u32[]{:S(2)}, u32[]{:S(2)}) collective-permute-start(bf16[256,128]{1,0:T(8,128)(2,1)S(1)} %get-tuple-element.65), channel_id=1, source_target_pairs={{0,3},{1,0},{2,1},{3,2},{4,7},{5,4},{6,5},{7,6},{8,11},{9,8},{10,9... | collective-permute-start | bytes 196616 | tf_op jit(solution)/shard_map/ppermute | solution.py:223
  143.0 6.1 %collective-permute-start.13 = (bf16[256,128]{1,0:T(8,128)(2,1)S(1)}, bf16[256,128]{1,0:T(8,128)(2,1)S(1)}, u32[]{:S(2)}, u32[]{:S(2)}) collective-permute-start(bf16[256,128]{1,0:T(8,128)(2,1)S(1)} %get-tuple-element.64), channel_id=1, source_target_pairs={{0,2},{1,3},{2,0},{3,1},{4,6},{5,7},{6,4},{7,5},{8,10},{9,11},{10,... | collective-permute-start | bytes 196616 | tf_op jit(solution)/shard_map/ppermute | solution.py:223
where the time goes:
time: 152 us; the launch traced here: 150 us
  Pallas kernels  53.5 us (35%)
  starting transfers between devices  43.2 us (28%)
  waiting for transfers between devices  21.9 us (14%)
  local copies, waits for them, and re-layouts  19.1 us (13%)
  other arithmetic  11.3 us (7%)
    pallas_call x4, Pallas kernels, main_group(): pl.pallas_call(functools.partial(main_kernel, not state), grid_spec=grid_...  48.6 us
    all_to_all x3, starting transfers between devices, all_to_all(): return lax.all_to_all(blocks, axis, 0, 0, tiled=True)  14.8 us
    all_to_all x3, waiting for transfers between devices, all_to_all(): return lax.all_to_all(blocks, axis, 0, 0, tiled=True)  13.1 us
    ppermute x6, starting transfers between devices, exchange(): got.append(lax.ppermute(sent, axis, ring(distance)))  12.2 us
    unnamed x43, local copies, waits for them, and re-layouts  12.1 us
    ppermute x6, waiting for transfers between devices, exchange(): got.append(lax.ppermute(sent, axis, ring(distance)))  5.95 us
    ppermute x1, starting transfers between devices, per_device(): lax.ppermute(own, both, [(2 * i + c, 2 * i + 2 + c) for i in range(3) for...  4.04 us
    dynamic_slice x2, local copies, waits for them, and re-layouts, other_half(): chosen = lax.dynamic_index_in_dim(parts, 1 - core, 1, keepdims=False)  3.87 us
  transfers between devices with their start and end apart: 21, of which 6 were waited for; matrix products, arithmetic and copies ran while one was open for 13% of the time, Pallas kernels for 19%

commit v1 on v0

--- a/solution.py
+++ b/solution.py
@@ -24,6 +24,7 @@
 KEYS = 2 * CHIP
 GROUP = 8
 PER_STEP = 4
+STEPS = GROUP // PER_STEP
 SCALE = 1.0 / math.sqrt(WIDTH)
 LOG2E = math.log2(math.e)
 NT = (((1,), (1,)), ((), ()))
@@ -34,23 +35,22 @@
     return lax.dot_general(a, b, dims, preferred_element_type=F32)
 
 
-def main_kernel(leading, *refs):
-    info, q_own, q_got, g_own, g_got, w_ref, lat_ref, latt_ref, rope_ref, low_ref = refs[:10]
-    dq_ref, send_ref, dw_ref, dlat_ref, drope_ref, bias_ref = refs[-6:]
+def main_kernel(groups, info, *refs):
+    q_own, q_got, g_own, g_got, w_ref, lat_ref, latt_ref, rope_ref, low_ref = refs[:9]
+    dlat_ref, drope_ref, bias_ref = refs[-3:]
+    dw_refs = refs[-3 - groups : -3]
+    dq_ref, send_ref = refs[-5 - groups : -3 - groups]
     first_core = info[0] == 0
-
-    @pl.when(pl.program_id(0) == 0)
+    step = pl.program_id(0)
+
+    @pl.when(step == 0)
     def _():
         key = lax.broadcasted_iota(jnp.int32, (KEYS, CHIP), 0)
         row = lax.broadcasted_iota(jnp.int32, (KEYS, CHIP), 1)
         ok = (key >= low_ref[...]) & (key <= row + CHIP)
         bias_ref[...] = jnp.where(ok, 0.0, -1e30)
-        if leading:
-            dlat_ref[...] = jnp.zeros_like(dlat_ref)
-            drope_ref[...] = jnp.zeros_like(drope_ref)
-        else:
-            dlat_ref[...] = refs[10][...]
-            drope_ref[...] = refs[11][...]
+        dlat_ref[...] = jnp.zeros_like(dlat_ref)
+        drope_ref[...] = jnp.zeros_like(drope_ref)
 
     rope = rope_ref[...]
     kv_all = mm(lat_ref[...], w_ref[...], NT).astype(BF16)
@@ -79,22 +79,33 @@
     drope_ref[...] += functools.reduce(jnp.add, dropes)
     dkv = jnp.concatenate(dkvs, axis=1)
     dw = mm(latt_ref[...], dkv).astype(BF16)
-    for j in range(2 * PER_STEP):
-        part = dw[:, j * 128 : (j + 1) * 128]
-        dw_ref[j // NZ, j % NZ] = part
+    for group, dw_ref in enumerate(dw_refs):
+
+        @pl.when(step // STEPS == group)
+        def _():
+            for j in range(2 * PER_STEP):
+                dw_ref[j // NZ, j % NZ] = dw[:, j * 128 : (j + 1) * 128]
+
     dlat_ref[...] += mm(dkv, w_ref[...])
 
 
-def main_group(info, q_full, q_got, g_full, g_got, w_kv, lat, latt, rope, low, state):
-    steps = GROUP // PER_STEP
-    half = lambda i, info: (info[1] * steps + i, 0, 0)
-    full = lambda i, info: ((2 * info[1] + info[0]) * steps + i, 0, 0)
+def main_groups(groups, info, q_full, q_got, g_full, g_got, w_kv, lat, latt, rope, low, held):
+    group_of = lambda i, info: info[1 + i // STEPS]
+    half = lambda i, info: (group_of(i, info) * STEPS + i % STEPS, 0, 0)
+    full = lambda i, info: ((2 * group_of(i, info) + info[0]) * STEPS + i % STEPS, 0, 0)
+    w_rows = lambda i, info: ((2 * group_of(i, info) + info[0]) * STEPS + i % STEPS, 0)
     whole = lambda i, info: (0, 0)
-    w_rows = lambda i, info: ((2 * info[1] + info[0]) * steps + i, 0)
     ys = 2 * PER_STEP // NZ
+
+    def dw_spec(group):
+        def index(i, info):
+            return (jnp.clip(i - group * STEPS, 0, STEPS - 1), 0, 0, 0)
+
+        return pl.BlockSpec((ys, NZ, LAT, 128), index)
+
     in_specs = [
         pl.BlockSpec((PER_STEP, WIDTH, ROWS), full),
-        pl.BlockSpec((PER_STEP, WIDTH, ROWS), half),
+        pl.BlockSpec((PER_STEP, WIDTH, ROWS), full),
         pl.BlockSpec((PER_STEP, ROWS, VDIM), full),
         pl.BlockSpec((PER_STEP, ROWS, VDIM), half),
         pl.BlockSpec((PER_STEP * HCOLS, LAT), w_rows),
@@ -104,47 +115,68 @@
         pl.BlockSpec((1, CHIP), whole),
     ]
     aliases = {}
-    if state:
-        in_specs += [
-            pl.BlockSpec((KEYS, LAT), whole),
-            pl.BlockSpec((KEYS, ROPE), whole),
-            pl.BlockSpec(memory_space=pl.ANY),
-            pl.BlockSpec(memory_space=pl.ANY),
-        ]
-        aliases = {12: 0, 13: 1}
+    if held:
+        in_specs += [pl.BlockSpec(memory_space=pl.ANY)] * 2
+        aliases = {10: 0, 11: 1}
     grid_spec = pltpu.PrefetchScalarGridSpec(
         num_scalar_prefetch=1,
-        grid=(steps,),
+        grid=(groups * STEPS,),
         in_specs=in_specs,
         out_specs=[
             pl.BlockSpec((PER_STEP, WIDTH, ROWS), full),
             pl.BlockSpec((PER_STEP, WIDTH, ROWS), half),
-            pl.BlockSpec((ys, NZ, LAT, 128), lambda i, info: (i, 0, 0, 0)),
-            pl.BlockSpec((KEYS, LAT), whole),
-            pl.BlockSpec((KEYS, ROPE), whole),
-        ],
+        ]
+        + [dw_spec(group) for group in range(groups)]
+        + [pl.BlockSpec((KEYS, LAT), whole), pl.BlockSpec((KEYS, ROPE), whole)],
         scratch_shapes=[pltpu.VMEM((KEYS, CHIP), F32)],
     )
-    flops = 2 * GROUP * KEYS * CHIP
-    return pl.pallas_call(
-        functools.partial(main_kernel, not state),
+    outs = pl.pallas_call(
+        functools.partial(main_kernel, groups),
         grid_spec=grid_spec,
         out_shape=[
             pltpu.HBM((HEADS, WIDTH, ROWS), BF16),
             pltpu.HBM((HEADS // 2, WIDTH, ROWS), BF16),
-            pltpu.HBM((4, 4, LAT, 128), BF16),
-            pltpu.HBM((KEYS, LAT), F32),
-            pltpu.HBM((KEYS, ROPE), F32),
-        ],
+        ]
+        + [pltpu.HBM((NY, NZ, LAT, 128), BF16)] * groups
+        + [pltpu.HBM((KEYS, LAT), F32), pltpu.HBM((KEYS, ROPE), F32)],
         input_output_aliases=aliases,
         compiler_params=pltpu.CompilerParams(
             dimension_semantics=("arbitrary",), vmem_limit_bytes=48 * 1024 * 1024
         ),
         cost_estimate=pl.CostEstimate(
-            flops=flops, bytes_accessed=10 * 1024 * 1024, transcendentals=0
+            flops=0, bytes_accessed=0, transcendentals=0
         ),
-        name="main_group",
-    )(info, q_full, q_got, g_full, g_got, w_kv, lat, latt, rope, low, *state)
+        name="main_groups",
+    )(info, q_full, q_got, g_full, g_got, w_kv, lat, latt, rope, low, *held)
+    return tuple(outs[:2]), outs[2 : 2 + groups], (outs[-2], outs[-1])
+
+
+def fold_kernel(*refs):
+    parts, (wide_ref, narrow_ref) = refs[:-2], refs[-2:]
+    dlat = functools.reduce(jnp.add, [ref[...] for ref in parts[0::2]])
+    drope = functools.reduce(jnp.add, [ref[...] for ref in parts[1::2]])
+    block = jnp.concatenate([dlat.T, drope.T], axis=0)
+    wide_ref[0] = block
+    narrow_ref[0] = block.astype(BF16)
+
+
+def fold(parts):
+    width = LAT + ROPE
+    rows = lambda j: (j, 0)
+    out = pl.BlockSpec((1, width, ROWS), lambda j: (j, 0, 0))
+    return pl.pallas_call(
+        fold_kernel,
+        grid=(KEYS // ROWS,),
+        in_specs=[pl.BlockSpec((ROWS, LAT), rows), pl.BlockSpec((ROWS, ROPE), rows)] * len(parts),
+        out_specs=[out, out],
+        out_shape=[
+            jax.ShapeDtypeStruct((4, width, ROWS), F32),
+            jax.ShapeDtypeStruct((4, width, ROWS), BF16),
+        ],
+        compiler_params=pltpu.CompilerParams(dimension_semantics=("arbitrary",)),
+        cost_estimate=pl.CostEstimate(flops=0, bytes_accessed=0, transcendentals=0),
+        name="fold",
+    )(*[array for pair in parts for array in pair])
 
 
 def window_kernel(info, own, mate, prev_same, prev_mate, lat_ref, latt_ref, rope_ref):
@@ -197,7 +229,7 @@
         out_shape=pltpu.HBM((HEADS, WIDTH, ROWS), BF16),
         input_output_aliases={2: 0},
         compiler_params=pltpu.CompilerParams(dimension_semantics=("arbitrary",)),
-        cost_estimate=pl.CostEstimate(flops=0, bytes_accessed=4 * 1024 * 1024, transcendentals=0),
+        cost_estimate=pl.CostEstimate(flops=0, bytes_accessed=0, transcendentals=0),
         name="place",
     )(info, got, held)
 
@@ -240,7 +272,6 @@
     x, core = lax.axis_index("x"), lax.axis_index("core")
     y, z = lax.axis_index("y"), lax.axis_index("z")
     swap = [(0, 1), (1, 0)]
-    both = ("x", "core")
     tie = lax.optimization_barrier
 
     def other_half(full):
@@ -250,12 +281,10 @@
 
     own = latent[0].T
     mate = lax.ppermute(own, "core", swap)
-    prev_same = lax.ppermute(own, both, [(2 * i + c, 2 * i + 2 + c) for i in range(3) for c in range(2)])
-    prev_mate = lax.ppermute(
-        own, both, [(2 * i + c, 2 * i + 2 + 1 - c) for i in range(3) for c in range(2)]
-    )
+    prev_same = lax.ppermute(own, "x", [(i, i + 1) for i in range(NX - 1)])
+    prev_mate = lax.ppermute(prev_same, "core", swap)
     q_full = query[0].transpose(1, 2, 0)
-    q_got = lax.ppermute(other_half(q_full), "core", swap)
+    q_got = lax.ppermute(q_full, "core", swap)
     g_full = tie(grad_out[0].transpose(1, 0, 2))
     g_got = lax.ppermute(other_half(g_full), "core", swap)
 
@@ -265,54 +294,36 @@
     starts = start_of(doc_lengths[0], base + jnp.arange(CHIP, dtype=jnp.int32))
     low = (starts - (base - CHIP)).astype(jnp.int32).reshape(1, CHIP)
 
-    def main(ahead, state):
-        group = lax.rem(x + ahead, NX)
-        info = jnp.stack([core, group]).astype(jnp.int32)
-        dq, send, dw, dlat, drope = main_group(
-            info, q_full, q_got, g_full, g_got, w_kv, lat, latt, rope, low, state
+    def main(held, *ahead):
+        info = jnp.stack([core] + [lax.rem(x + n, NX) for n in ahead]).astype(jnp.int32)
+        return main_groups(
+            len(ahead), info, q_full, q_got, g_full, g_got, w_kv, lat, latt, rope, low, held
         )
-        return dw, (dlat, drope, dq, send)
-
-    dw, state = main(1, ())
-    from_left = lax.ppermute(dw, "x", ring(1))
-    dw, state = main(3, state)
-    from_right = lax.ppermute(dw, "x", ring(3))
-    dw, state = main(2, state)
-    across = all_to_all(dw, "y")
-    dw, state = main(0, state)
-    dlat, drope, dq, send = state
-
-    across = summed(across)
-    mine = total([dw, from_left, from_right]).astype(BF16)
-    part_a = all_to_all(mine[:, :, : LAT // 2], "y")
-    rows_b = NY * LAT // 2
-    part_b = jnp.swapaxes(mine[:, :, LAT // 2 :], 0, 1).reshape(NZ, rows_b, 128)
-    part_b = total(exchange(jnp.concatenate([part_b, across], axis=1), "z", z))
-    across = lax.ppermute(part_b[rows_b:].astype(BF16), "x", ring(2))
-    part_b = part_b[:rows_b].astype(BF16).reshape(NY, LAT // 2, 128)
-    part_b = all_to_all(part_b, "y")
-    part_a = total(exchange(summed(part_a), "z", z))
-    part_b = jnp.sum(part_b.astype(F32), axis=0)
-    d_weight = (jnp.concatenate([part_a, part_b], axis=0) + across.astype(F32)).T
-
-    terms = jnp.concatenate([dlat, drope], axis=-1)
-    blocks = terms.reshape(4, ROWS, LAT + ROPE)
-    mine = pick(blocks, 2 + core)
-    from_mate = lax.ppermute(pick(blocks, 3 - core).astype(BF16), "core", swap)
-    from_next = lax.ppermute(
-        pick(blocks, core).astype(BF16),
-        both,
-        [(2 * i + 2 + c, 2 * i + c) for i in range(3) for c in range(2)],
-    )
-    from_next_mate = lax.ppermute(
-        pick(blocks, 1 - core).astype(BF16),
-        both,
-        [(2 * i + 2 + c, 2 * i + 1 - c) for i in range(3) for c in range(2)],
-    )
-    d_latent = total([mine, from_mate, from_next, from_next_mate]).astype(BF16)
+
+    held, (dw_left, dw_right), part_0 = main((), 1, 3)
+    from_left = lax.ppermute(dw_left, "x", ring(1))
+    from_right = lax.ppermute(dw_right, "x", ring(3))
+    held, (dw_far,), part_1 = main(held, 2)
+    across = all_to_all(dw_far.reshape(NY * NZ, LAT, 128), ("y", "z"))
+    (dq, send), (dw_own,), part_2 = main(held, 0)
 
     got = lax.ppermute(send, "core", swap)
+    wide, narrow = fold((part_0, part_1, part_2))
+    wide = wide.reshape(2, NCORE, LAT + ROPE, ROWS)
+    narrow = narrow.reshape(2, NCORE, LAT + ROPE, ROWS)
+    prev_sum, own_sum = lax.dynamic_index_in_dim(wide, core, 1, keepdims=False)
+    give = lax.dynamic_index_in_dim(narrow, 1 - core, 1, keepdims=False)
+    taken = lax.ppermute(give, "core", swap)
+    prev_sum = (prev_sum + taken[0].astype(F32)).astype(BF16)
     d_query = place(core_info, got, dq)
+
+    across = lax.ppermute(summed(across), "x", ring(2))
+    mine = total([dw_own, from_left, from_right]).astype(BF16)
+    mine = all_to_all(mine.reshape(NY * NZ, LAT, 128), ("y", "z"))
+    from_next = lax.ppermute(prev_sum, "x", [(i + 1, i) for i in range(NX - 1)])
+    d_latent = total([own_sum, taken[1], from_next]).astype(BF16).T
+    d_weight = (jnp.sum(mine.astype(F32), axis=0) + across.astype(F32)).T
+
     return (d_query.transpose(2, 0, 1)[None], d_latent[None], d_weight)
 
 

time: 152 us -> 133 us (0.88)
  starting transfers between devices: 43.2 us -> 30.3 us
  local copies, waits for them, and re-layouts: 19.1 us -> 10 us
  Pallas kernels: 53.5 us -> 56.4 us
  waiting for transfers between devices: 21.9 us -> 23.9 us
    ppermute x15 -> x8, starting transfers between devices: 27.8 us -> 13 us  [the longest x1 4.04 us: per_device(): prev_same = lax.ppermute(own, 'x', [(i, i + 1) for i in range(NX - 1)])]
    ppermute x15 -> x8, waiting for transfers between devices: 8.78 us -> 23.1 us  [the longest x1 8.3 us: per_device(): from_left = lax.ppermute(dw_left, 'x', ring(1))]
    all_to_all x3 -> x2, waiting for transfers between devices: 13.1 us -> 0.76 us  [all_to_all(): return lax.all_to_all(blocks, axis, 0, 0, tiled=True)]
    unnamed x43 -> x18, local copies, waits for them, and re-layouts: 12.1 us -> 7.96 us
    convert_element_type x1 -> x2, other arithmetic: 3.05 us -> 6.1 us  [the longest x1 5.1 us: per_device(): mine = total([dw_own, from_left, from_right]).astype(BF16)]
    pallas_call x4, Pallas kernels: 48.6 us -> 51.5 us  [the longest x3 47.2 us: main_groups(): pl.pallas_call(functools.partial(main_kernel, groups), grid_spec=grid_spe...]
    dynamic_slice x2 -> x1, local copies, waits for them, and re-layouts: 3.87 us -> 1.05 us  [other_half(): chosen = lax.dynamic_index_in_dim(parts, 1 - core, 1, keepdims=False)]
    all_to_all x3 -> x2, starting transfers between devices: 14.8 us -> 16.8 us  [all_to_all(): return lax.all_to_all(blocks, axis, 0, 0, tiled=True)]
  transfers between devices with their start and end apart: 21 -> 13, of which waited for: 6 -> 8; matrix products, arithmetic and copies ran while one was open for 13% -> 12% of each run, Pallas kernels for 19% -> 26%
where the time goes in v1:
time: 133 us; the launch traced here: 132 us
  Pallas kernels  56.4 us (42%)
  starting transfers between devices  30.3 us (23%)
  waiting for transfers between devices  23.9 us (18%)
  other arithmetic  10.4 us (8%)
  local copies, waits for them, and re-layouts  10 us (8%)
    pallas_call x3, Pallas kernels, main_groups(): pl.pallas_call(functools.partial(main_kernel, groups), grid_spec=grid_spe...  47.2 us
    all_to_all x2, starting transfers between devices, all_to_all(): return lax.all_to_all(blocks, axis, 0, 0, tiled=True)  16.8 us
    ppermute x1, waiting for transfers between devices, per_device(): from_left = lax.ppermute(dw_left, 'x', ring(1))  8.3 us
    unnamed x18, local copies, waits for them, and re-layouts  7.96 us
    ppermute x1, waiting for transfers between devices, per_device(): from_next = lax.ppermute(prev_sum, 'x', [(i + 1, i) for i in range(NX - 1)])  6.72 us
    convert_element_type x1, other arithmetic, per_device(): mine = total([dw_own, from_left, from_right]).astype(BF16)  5.1 us
    pallas_call x1, Pallas kernels, fold(): pl.pallas_call(fold_kernel, grid=(KEYS // ROWS,), in_specs=[pl.BlockSpec(...  4.28 us
    ppermute x1, starting transfers between devices, per_device(): prev_same = lax.ppermute(own, 'x', [(i, i + 1) for i in range(NX - 1)])  4.04 us
  transfers between devices with their start and end apart: 13, of which 8 were waited for; matrix products, arithmetic and copies ran while one was open for 12% of the time, Pallas kernels for 26%

profile of v1, /device:TPU:8, one launch (start us, length us, event | category | flops | bytes accessed | tf_op | source)
XLA Modules:
  0.0 131.7 jit_solution(14389488768667919992)
XLA Ops:
  0.6 0.1 collective-permute-start
  0.7 2.9 %copy.23 = bf16[1,128,64,128]{3,1,2,0:T(8,128)(2,1)S(1)} copy(bf16[1,128,64,128]{3,2,1,0:T(8,128)(2,1)} %param.9) | data formatting | bytes 4194304 | tf_op args[4]
  3.7 0.0 copy-start.6
  3.7 0.0 copy-start.7
  3.7 1.0 constant_dynamic-slice_fusion
  4.8 0.5 collective-permute-start.1
  5.2 4.0 %collective-permute-start.3 = (bf16[576,128]{1,0:T(8,128)(2,1)S(1)}, bf16[576,128]{1,0:T(8,128)(2,1)}, u32[]{:S(2)}, u32[]{:S(2)}) collective-permute-start(bf16[576,128]{1,0:T(8,128)(2,1)S(1)} %bitcast.69), channel_id=1, source_target_pairs={{0,32},{32,64},{64,96},{1,33},{33,65},{65,97},{2,34},{34,66},{66,9... | collective-permute-start | bytes 442376 | tf_op jit(solution)/shard_map/ppermute | solution.py:284
  9.3 0.2 reduce-window.8
  9.5 0.1 select_reduce_fusion
  9.6 2.3 %collective-permute-done.3.prev_same = bf16[576,128]{1,0:T(8,128)(2,1)} collective-permute-done((bf16[576,128]{1,0:T(8,128)(2,1)S(1)}, bf16[576,128]{1,0:T(8,128)(2,1)}, u32[]{:S(2)}, u32[]{:S(2)}) %collective-permute-start.3) | collective-permute-done | bytes 147488 | tf_op jit(solution)/shard_map/ppermute | solution.py:284
  11.9 0.1 pad_add_fusion.2.info
  12.0 0.0 collective-permute-done.2.mate
  12.0 1.6 %collective-permute-done.4.prev_mate = bf16[576,128]{1,0:T(8,128)(2,1)} collective-permute-done((bf16[576,128]{1,0:T(8,128)(2,1)}, bf16[576,128]{1,0:T(8,128)(2,1)}, u32[]{:S(2)}, u32[]{:S(2)}) %collective-permute-start.4) | collective-permute-done | bytes 147488 | tf_op jit(solution)/shard_map/ppermute | solution.py:285
  13.6 1.3 window.1
  14.9 0.0 collective-permute-done.1.refs_3_
  15.0 0.0 collective-permute-done.refs_1_
  15.0 22.2 %main_groups.3 = (bf16[64,192,128]{2,1,0:T(8,128)(2,1)}, bf16[32,192,128]{2,1,0:T(8,128)(2,1)}, bf16[4,4,512,128]{3,2,1,0:T(8,128)(2,1)}, bf16[4,4,512,128]{3,2,...) custom-call(s32[3]{0:T(128)S(1)} %pad_add_fusion.2.info, bf16[64,192,128]{2,1,0:T(8,128)(2,1)} %bitcast.76, ...), custom_call_target="tpu_custom_call" | custom-call | tf_op jit(solution)/shard_map/main_groups/pallas_call | solution.py:133
  37.2 2.7 %collective-permute-start.8 = (bf16[4,4,512,128]{3,2,1,0:T(8,128)(2,1)}, bf16[4,4,512,128]{3,2,1,0:T(8,128)(2,1)}, u32[]{:S(2)}, u32[]{:S(2)}) collective-permute-start(bf16[4,4,512,128]{3,2,1,0:T(8,128)(2,1)} %get-tuple-element.42), channel_id=1, source_target_pairs={{0,32},{32,64},{64,96},{96,0},{1,33},{33,65},{65,97},{97,1},{2,34}... | collective-permute-start | bytes 6291464 | tf_op jit(solution)/shard_map/ppermute | solution.py:304
  39.9 1.5 %collective-permute-start.9 = (bf16[4,4,512,128]{3,2,1,0:T(8,128)(2,1)}, bf16[4,4,512,128]{3,2,1,0:T(8,128)(2,1)}, u32[]{:S(2)}, u32[]{:S(2)}) collective-permute-start(bf16[4,4,512,128]{3,2,1,0:T(8,128)(2,1)} %get-tuple-element.43), channel_id=1, source_target_pairs={{0,96},{32,0},{64,32},{96,64},{1,97},{33,1},{65,33},{97,65},{2,98}... | collective-permute-start | bytes 6291464 | tf_op jit(solution)/shard_map/ppermute | solution.py:305
  41.4 0.1 pad_add_fusion
  41.5 1.0 copy-done.1
  42.5 1.0 copy-done.4
  43.6 12.5 %main_groups.4 = (bf16[64,192,128]{2,1,0:T(8,128)(2,1)}, bf16[32,192,128]{2,1,0:T(8,128)(2,1)}, bf16[4,4,512,128]{3,2,1,0:T(8,128)(2,1)}, f32[512,512]{1,0:T(8,128)}, f32[512,64]{1,0:T(8,128)}) custom-call(s32[2]{0:T(128)S(1)} %get-tuple-element.52.info, bf16[64,192,128]{2,1,0:T(8,128)(2,1)} %bitcast.77, ...), custom_call_target="tpu_custom_call", output_to_operand_aliasing={{0}: (10, {}), {1}: (11, {})} | custom-call | tf_op jit(solution)/shard_map/main_groups/pallas_call | solution.py:133
  56.1 8.4 %all-to-all-start.1 = ((bf16[16,512,128]{2,1,0:T(8,128)(2,1)}), bf16[16,512,128]{2,1,0:T(8,128)(2,1)}, u32[]{:S(2)}, u32[]{:S(2)}) async-start(bf16[16,512,128]{2,1,0:T(8,128)(2,1)} %bitcast.81), calls=%async_computation.1 | async-start | bytes 4194304 | tf_op jit(solution)/shard_map/all_to_all | solution.py:264
  64.5 1.0 copy-done.2
  65.5 1.0 copy-done.5
  66.6 12.5 %main_groups.5 = (bf16[64,192,128]{2,1,0:T(8,128)(2,1)}, bf16[32,192,128]{2,1,0:T(8,128)(2,1)}, bf16[4,4,512,128]{3,2,1,0:T(8,128)(2,1)}, f32[512,512]{1,0:T(8,128)}, f32[512,64]{1,0:T(8,128)}) custom-call(s32[2]{0:T(128)S(1)} %get-tuple-element.51.info, bf16[64,192,128]{2,1,0:T(8,128)(2,1)} %bitcast.78, ...), custom_call_target="tpu_custom_call", output_to_operand_aliasing={{0}: (10, {}), {1}: (11, {})} | custom-call | tf_op jit(solution)/shard_map/main_groups/pallas_call | solution.py:133
  79.1 8.3 %collective-permute-done.8 = bf16[4,4,512,128]{3,2,1,0:T(8,128)(2,1)} collective-permute-done((bf16[4,4,512,128]{3,2,1,0:T(8,128)(2,1)}, bf16[4,4,512,128]{3,2,1,0:T(8,128)(2,1)}, u32[]{:S(2)}, u32[]{:S(2)}) %collective-permute-start.8) | collective-permute-done | bytes 2097184 | tf_op jit(solution)/shard_map/ppermute | solution.py:304
  87.4 0.2 collective-permute-done.9
  87.6 5.1 %add_convert_fusion = bf16[4,4,512,128]{3,2,1,0:T(8,128)(2,1)} fusion(bf16[4,4,512,128]{3,2,1,0:T(8,128)(2,1)} %collective-permute-done.9, bf16[4,4,512,128]{3,2,1,0:T(8,128)(2,1)} %collective-permute-done.8, bf16[4,4,512,128]{3,2,1,0:T(8,128)(2,1)} %get-tuple-element.41), kind=kLoop, calls=%fused_computation.1 | loop fusion | flops 6291456 | bytes 8388608 | tf_op jit(solution)/shard_map/convert_element_type | solution.py:321
  92.7 0.0 all-to-all-done.1
  92.7 8.4 %all-to-all-start = ((bf16[16,512,128]{2,1,0:T(8,128)(2,1)}), bf16[16,512,128]{2,1,0:T(8,128)(2,1)S(1)}, u32[]{:S(2)}, u32[]{:S(2)}) async-start(bf16[16,512,128]{2,1,0:T(8,128)(2,1)} %bitcast.80), calls=%async_computation | async-start | bytes 4194304 | tf_op jit(solution)/shard_map/all_to_all | solution.py:264
  101.1 0.0 collective-permute-start.5
  101.1 4.3 %fold.1 = (f32[4,576,128]{2,1,0:T(8,128)}, bf16[4,576,128]{2,1,0:T(8,128)(2,1)}) custom-call(f32[512,512]{1,0:T(8,128)} %get-tuple-element.33.refs_0_, f32[512,64]{1,0:T(8,128)} %get-tuple-element.34.refs_1_, f32[512,512]{1,0:T(8,128)} %get-tuple-element.35.refs_2_, f32[512,64]{1,0:T(8,128)} %get-tuple-element.36.refs_3_, ...), custom_call_target="tpu_custom_call" | custom-call | tf_op jit(solution)/shard_map/fold/pallas_call | solution.py:167
  105.4 1.0 dynamic-slice_bitcast_fusion.2
  106.4 0.6 collective-permute-start.6
  106.9 1.2 collective-permute-done.6
  108.2 1.0 fusion.1
  109.1 1.3 collective-permute-start.7
  110.4 6.7 %collective-permute-done.7 = bf16[576,128]{1,0:T(8,128)(2,1)S(1)} collective-permute-done((bf16[576,128]{1,0:T(8,128)(2,1)S(1)}, bf16[576,128]{1,0:T(8,128)(2,1)S(1)}, u32[]{:S(2)}, u32[]{:S(2)}) %collective-permute-start.7) | collective-permute-done | bytes 147488 | tf_op jit(solution)/shard_map/ppermute | solution.py:323
  117.2 1.7 %fusion.5 = bf16[1,128,576]{1,2,0:T(8,128)(2,1)} fusion(bf16[576,128]{1,0:T(8,128)(2,1)S(1)} %collective-permute-done.7, f32[2,2,576,128]{3,2,1,0:T(8,128)} %bitcast.83, s32[]{:T(128)S(6)} %add.66, s32[]{:T(128)S(6)} %select_n.16, bf16[2,576,128]{2,1,0:T(8,128)(2,1)S(1)} %collective-permute-done.6), kind=kLoop, calls=%fused_computation.12 | loop fusion | flops 368640 | bytes 737288 | tf_op jit(solution)/shard_map/broadcast_in_dim | solution.py:327
  118.8 3.6 %place.1 = bf16[64,192,128]{2,1,0:T(8,128)(2,1)} custom-call(s32[1]{0:T(128)} %bitcast.info, bf16[32,192,128]{2,1,0:T(8,128)(2,1)} %collective-permute-done.5.got_ref, bf16[64,192,128]{2,1,0:T(8,128)(2,1)} %get-tuple-element.32.held_ref), custom_call_target="tpu_custom_call", output_to_operand_aliasing={{}: (2, {})} | custom-call | tf_op jit(solution)/shard_map/place/pallas_call | solution.py:226
  122.4 1.9 %reduce_sum.32 = bf16[512,128]{1,0:T(8,128)(2,1)S(1)} reduce(bf16[16,512,128]{2,1,0:T(8,128)(2,1)} %all-to-all-done.1, bf16[]{:T(256)} %constant.52.clone.1), dimensions={0}, to_apply=%region_3.4 | reduce | flops 983040 | bytes 2228226 | tf_op jit(solution)/shard_map/reduce_sum | solution.py:268
  124.3 2.8 %collective-permute-start.10 = (bf16[512,128]{1,0:T(8,128)(2,1)S(1)}, bf16[512,128]{1,0:T(8,128)(2,1)S(1)}, u32[]{:S(2)}, u32[]{:S(2)}) collective-permute-start(bf16[512,128]{1,0:T(8,128)(2,1)S(1)} %reduce_sum.32), channel_id=1, source_target_pairs={{0,64},{32,96},{64,0},{96,32},{1,65},{33,97},{65,1},{97,33},{2,66}... | collective-permute-start | bytes 393224 | tf_op jit(solution)/shard_map/ppermute | solution.py:320
  127.1 0.8 all-to-all-done
  127.9 0.3 convert_reduce_fusion
  128.2 2.7 %collective-permute-done.10 = bf16[512,128]{1,0:T(8,128)(2,1)S(1)} collective-permute-done((bf16[512,128]{1,0:T(8,128)(2,1)S(1)}, bf16[512,128]{1,0:T(8,128)(2,1)S(1)}, u32[]{:S(2)}, u32[]{:S(2)}) %collective-permute-start.10) | collective-permute-done | bytes 131104 | tf_op jit(solution)/shard_map/ppermute | solution.py:320
  130.9 0.8 copy.20
  (16 shorter events, 0.1 us)
Async XLA Ops:
  0.6 14.3 %collective-permute-start = (bf16[64,192,128]{2,1,0:T(8,128)(2,1)}, bf16[64,192,128]{2,1,0:T(8,128)(2,1)}, u32[]{:S(2)}, u32[]{:S(2)}) collective-permute-start(bf16[64,192,128]{2,1,0:T(8,128)(2,1)} %bitcast.75), channel_id=1, source_target_pairs={{0,16},{16,0},{1,17},{17,1},{2,18},{18,2},{3,19},{19,3},{4,20},{20... | collective-permute-start | bytes 9437192 | tf_op jit(solution)/shard_map/ppermute | solution.py:287
  3.7 1.6 %copy-start.6 = (bf16[1,128,576]{1,2,0:T(8,128)(2,1)S(1)}, bf16[1,128,576]{1,2,0:T(8,128)(2,1)}, u32[]{:S(2)}) copy-start(bf16[1,128,576]{1,2,0:T(8,128)(2,1)} %param.6) | copy-start | bytes 442372
  3.7 5.6 %copy-start.7 = (s32[1,8]{1,0:T(1,128)S(1)}, s32[1,8]{1,0:T(1,128)}, u32[]{:S(2)}) copy-start(s32[1,8]{1,0:T(1,128)} %param.7) | copy-start | bytes 100
  4.8 10.2 %collective-permute-start.1 = (bf16[32,128,128]{2,1,0:T(8,128)(2,1)}, bf16[32,128,128]{2,1,0:T(8,128)(2,1)S(1)}, u32[]{:S(2)}, u32[]{:S(2)}) collective-permute-start(bf16[32,128,128]{2,1,0:T(8,128)(2,1)} %bitcast.8), channel_id=1, source_target_pairs={{0,16},{16,0},{1,17},{17,1},{2,18},{18,2},{3,19},{19,3},{4,20},{20... | collective-permute-start | bytes 3145736 | tf_op jit(solution)/shard_map/ppermute | solution.py:289
  5.2 6.7 %collective-permute-start.3 = (bf16[576,128]{1,0:T(8,128)(2,1)S(1)}, bf16[576,128]{1,0:T(8,128)(2,1)}, u32[]{:S(2)}, u32[]{:S(2)}) collective-permute-start(bf16[576,128]{1,0:T(8,128)(2,1)S(1)} %bitcast.69), channel_id=1, source_target_pairs={{0,32},{32,64},{64,96},{1,33},{33,65},{65,97},{2,34},{34,66},{66,9... | collective-permute-start | bytes 442376 | tf_op jit(solution)/shard_map/ppermute | solution.py:284
  9.3 2.7 %collective-permute-start.2 = (bf16[576,128]{1,0:T(8,128)(2,1)S(1)}, bf16[576,128]{1,0:T(8,128)(2,1)}, u32[]{:S(2)}, u32[]{:S(2)}) collective-permute-start(bf16[576,128]{1,0:T(8,128)(2,1)S(1)} %bitcast.70), channel_id=1, source_target_pairs={{0,16},{16,0},{1,17},{17,1},{2,18},{18,2},{3,19},{19,3},{4,20},{20... | collective-permute-start | bytes 442376 | tf_op jit(solution)/shard_map/ppermute | solution.py:283
  11.9 1.7 %collective-permute-start.4 = (bf16[576,128]{1,0:T(8,128)(2,1)}, bf16[576,128]{1,0:T(8,128)(2,1)}, u32[]{:S(2)}, u32[]{:S(2)}) collective-permute-start(bf16[576,128]{1,0:T(8,128)(2,1)} %collective-permute-done.3.prev_same), channel_id=1, source_target_pairs={{0,16},{16,0},{1,17},{17,1},{2,18},{18,2},{3,19},{19,3},{4,20},{20... | collective-permute-start | bytes 442376 | tf_op jit(solution)/shard_map/ppermute | solution.py:285
  14.9 22.3 %copy-start = (bf16[512,512]{1,0:T(8,128)(2,1)}, bf16[512,512]{1,0:T(8,128)(2,1)S(1)}, u32[]{:S(2)}) copy-start(bf16[512,512]{1,0:T(8,128)(2,1)S(1)} %get-tuple-element.24.refs_5_) | copy-start | bytes 1572868
  14.9 22.3 %copy-start.3 = (bf16[512,512]{1,0:T(8,128)(2,1)}, bf16[512,512]{1,0:T(8,128)(2,1)S(1)}, u32[]{:S(2)}) copy-start(bf16[512,512]{1,0:T(8,128)(2,1)S(1)} %get-tuple-element.25.refs_6_) | copy-start | bytes 1572868
  37.2 50.2 %collective-permute-start.8 = (bf16[4,4,512,128]{3,2,1,0:T(8,128)(2,1)}, bf16[4,4,512,128]{3,2,1,0:T(8,128)(2,1)}, u32[]{:S(2)}, u32[]{:S(2)}) collective-permute-start(bf16[4,4,512,128]{3,2,1,0:T(8,128)(2,1)} %get-tuple-element.42), channel_id=1, source_target_pairs={{0,32},{32,64},{64,96},{96,0},{1,33},{33,65},{65,97},{97,1},{2,34}... | collective-permute-start | bytes 6291464 | tf_op jit(solution)/shard_map/ppermute | solution.py:304
  39.9 47.7 %collective-permute-start.9 = (bf16[4,4,512,128]{3,2,1,0:T(8,128)(2,1)}, bf16[4,4,512,128]{3,2,1,0:T(8,128)(2,1)}, u32[]{:S(2)}, u32[]{:S(2)}) collective-permute-start(bf16[4,4,512,128]{3,2,1,0:T(8,128)(2,1)} %get-tuple-element.43), channel_id=1, source_target_pairs={{0,96},{32,0},{64,32},{96,64},{1,97},{33,1},{65,33},{97,65},{2,98}... | collective-permute-start | bytes 6291464 | tf_op jit(solution)/shard_map/ppermute | solution.py:305
  41.5 1.0 copy-start.1
  42.5 1.0 copy-start.4
  56.1 36.6 %all-to-all-start.1 = ((bf16[16,512,128]{2,1,0:T(8,128)(2,1)}), bf16[16,512,128]{2,1,0:T(8,128)(2,1)}, u32[]{:S(2)}, u32[]{:S(2)}) async-start(bf16[16,512,128]{2,1,0:T(8,128)(2,1)} %bitcast.81), calls=%async_computation.1 | async-start | bytes 4194304 | tf_op jit(solution)/shard_map/all_to_all | solution.py:264
  64.5 1.0 copy-start.2
  65.5 1.0 copy-start.5
  92.7 35.2 %all-to-all-start = ((bf16[16,512,128]{2,1,0:T(8,128)(2,1)}), bf16[16,512,128]{2,1,0:T(8,128)(2,1)S(1)}, u32[]{:S(2)}, u32[]{:S(2)}) async-start(bf16[16,512,128]{2,1,0:T(8,128)(2,1)} %bitcast.80), calls=%async_computation | async-start | bytes 4194304 | tf_op jit(solution)/shard_map/all_to_all | solution.py:264
  101.1 17.7 %collective-permute-start.5 = (bf16[32,192,128]{2,1,0:T(8,128)(2,1)}, bf16[32,192,128]{2,1,0:T(8,128)(2,1)}, u32[]{:S(2)}, u32[]{:S(2)}) collective-permute-start(bf16[32,192,128]{2,1,0:T(8,128)(2,1)} %get-tuple-element.31), channel_id=1, source_target_pairs={{0,16},{16,0},{1,17},{17,1},{2,18},{18,2},{3,19},{19,3},{4,20},{20... | collective-permute-start | bytes 4718600 | tf_op jit(solution)/shard_map/ppermute | solution.py:310
  106.4 1.8 %collective-permute-start.6 = (bf16[2,576,128]{2,1,0:T(8,128)(2,1)S(1)}, bf16[2,576,128]{2,1,0:T(8,128)(2,1)S(1)}, u32[]{:S(2)}, u32[]{:S(2)}) collective-permute-start(bf16[2,576,128]{2,1,0:T(8,128)(2,1)S(1)} %dynamic-slice_bitcast_fusion.2), channel_id=1, source_target_pairs={{0,16},{16,0},{1,17},{17,1},{2,18},{18,2},{3,19},{19,3},{4,20},{20... | collective-permute-start | bytes 884744 | tf_op jit(solution)/shard_map/ppermute | solution.py:316
  109.1 8.0 %collective-permute-start.7 = (bf16[576,128]{1,0:T(8,128)(2,1)S(1)}, bf16[576,128]{1,0:T(8,128)(2,1)S(1)}, u32[]{:S(2)}, u32[]{:S(2)}) collective-permute-start(bf16[576,128]{1,0:T(8,128)(2,1)S(1)} %fusion.1), channel_id=1, source_target_pairs={{32,0},{64,32},{96,64},{33,1},{65,33},{97,65},{34,2},{66,34},{98,6... | collective-permute-start | bytes 442376 | tf_op jit(solution)/shard_map/ppermute | solution.py:323
  124.3 6.6 %collective-permute-start.10 = (bf16[512,128]{1,0:T(8,128)(2,1)S(1)}, bf16[512,128]{1,0:T(8,128)(2,1)S(1)}, u32[]{:S(2)}, u32[]{:S(2)}) collective-permute-start(bf16[512,128]{1,0:T(8,128)(2,1)S(1)} %reduce_sum.32), channel_id=1, source_target_pairs={{0,64},{32,96},{64,0},{96,32},{1,65},{33,97},{65,1},{97,33},{2,66}... | collective-permute-start | bytes 393224 | tf_op jit(solution)/shard_map/ppermute | solution.py:320

commit v2 on v1

--- a/solution.py
+++ b/solution.py
@@ -54,7 +54,7 @@
 
     rope = rope_ref[...]
     kv_all = mm(lat_ref[...], w_ref[...], NT).astype(BF16)
-    dkvs, dropes = [], []
+    fronts = []
     for i in range(PER_STEP):
         qo, qr, go, gr = q_own[i], q_got[i], g_own[i], g_got[i]
         q = jnp.concatenate([jnp.where(first_core, qo, qr), jnp.where(first_core, qr, qo)], axis=1)
@@ -63,17 +63,20 @@
         k = jnp.concatenate([kv_all[:, col : col + NOPE], rope], axis=1)
         v = kv_all[:, col + NOPE : col + HCOLS]
         s = mm(k, q) * (SCALE * LOG2E) + bias_ref[...]
+        dp = mm(v, g, NT)
         e = jnp.exp2(s - jnp.max(s, axis=0, keepdims=True))
         r = 1.0 / jnp.sum(e, axis=0, keepdims=True)
-        dp = mm(v, g, NT)
         delta = jnp.sum(e * dp, axis=0, keepdims=True) * r
         rs = r * SCALE
         ds = (e * (dp * rs - delta * rs)).astype(BF16)
+        fronts.append((q, g, k, ds, (e * r).astype(BF16)))
+    dkvs, dropes = [], []
+    for i, (q, g, k, ds, p) in enumerate(fronts):
         dq = mm(k, ds, TN).astype(BF16)
         dq_ref[i] = jnp.where(first_core, dq[:, :ROWS], dq[:, ROWS:])
         send_ref[i] = jnp.where(first_core, dq[:, ROWS:], dq[:, :ROWS])
         dk = mm(ds, q, NT)
-        dv = mm((e * r).astype(BF16), g)
+        dv = mm(p, g)
         dropes.append(dk[:, NOPE:])
         dkvs.append(jnp.concatenate([dk[:, :NOPE], dv], axis=1).astype(BF16))
     drope_ref[...] += functools.reduce(jnp.add, dropes)
@@ -282,13 +285,14 @@
     own = latent[0].T
     mate = lax.ppermute(own, "core", swap)
     prev_same = lax.ppermute(own, "x", [(i, i + 1) for i in range(NX - 1)])
-    prev_mate = lax.ppermute(prev_same, "core", swap)
     q_full = query[0].transpose(1, 2, 0)
     q_got = lax.ppermute(q_full, "core", swap)
     g_full = tie(grad_out[0].transpose(1, 0, 2))
+    prev_same, mate, g_full = tie((prev_same, mate, g_full))
     g_got = lax.ppermute(other_half(g_full), "core", swap)
 
     core_info = core.astype(jnp.int32).reshape(1)
+    prev_mate = lax.ppermute(prev_same, "core", swap)
     lat, latt, rope = window_of(core_info, (own, mate, prev_same, prev_mate))
     base = x * CHIP
     starts = start_of(doc_lengths[0], base + jnp.arange(CHIP, dtype=jnp.int32))

time: 133 us -> 131 us (0.985)
  Pallas kernels: 56.4 us -> 52.2 us
  local copies, waits for them, and re-layouts: 10 us -> 11.8 us
    pallas_call x3, Pallas kernels: 47.2 us -> 43.2 us  [main_groups(): pl.pallas_call(functools.partial(main_kernel, groups), grid_spec=grid_spe...]
    ppermute x1, waiting for transfers between devices: 8.3 us -> 10.5 us  [per_device(): from_left = lax.ppermute(dw_left, 'x', ring(1))]
    unnamed x18 -> x26, local copies, waits for them, and re-layouts: 7.96 us -> 9.79 us
    ppermute x1, waiting for transfers between devices: 2.34 us -> 0.79 us  [per_device(): prev_same = lax.ppermute(own, 'x', [(i, i + 1) for i in range(NX - 1)])]
  transfers between devices with their start and end apart: 13 -> 13, of which waited for: 8 -> 8; matrix products, arithmetic and copies ran while one was open for 12% -> 12% of each run, Pallas kernels for 26% -> 25%
where the time goes in v2:
time: 131 us; the launch traced here: 130 us
  Pallas kernels  52.2 us (40%)
  starting transfers between devices  29.6 us (23%)
  waiting for transfers between devices  25 us (19%)
  local copies, waits for them, and re-layouts  11.8 us (9%)
  other arithmetic  10.4 us (8%)
    pallas_call x3, Pallas kernels, main_groups(): pl.pallas_call(functools.partial(main_kernel, groups), grid_spec=grid_spe...  43.2 us
    all_to_all x2, starting transfers between devices, all_to_all(): return lax.all_to_all(blocks, axis, 0, 0, tiled=True)  16.8 us
    ppermute x1, waiting for transfers between devices, per_device(): from_left = lax.ppermute(dw_left, 'x', ring(1))  10.5 us
    unnamed x26, local copies, waits for them, and re-layouts  9.79 us
    ppermute x1, waiting for transfers between devices, per_device(): from_next = lax.ppermute(prev_sum, 'x', [(i + 1, i) for i in range(NX - 1)])  6.72 us
    convert_element_type x1, other arithmetic, per_device(): mine = total([dw_own, from_left, from_right]).astype(BF16)  5.09 us
    pallas_call x1, Pallas kernels, fold(): pl.pallas_call(fold_kernel, grid=(KEYS // ROWS,), in_specs=[pl.BlockSpec(...  4.31 us
    pallas_call x1, Pallas kernels, place(): pl.pallas_call(place_kernel, grid_spec=grid_spec, out_shape=pltpu.HBM((HE...  3.56 us
  transfers between devices with their start and end apart: 13, of which 8 were waited for; matrix products, arithmetic and copies ran while one was open for 12% of the time, Pallas kernels for 25%

profile of v2, /device:TPU:8, one launch (start us, length us, event | category | flops | bytes accessed | tf_op | source)
XLA Modules:
  0.0 129.8 jit_solution(5914972945126555181)
XLA Ops:
  0.6 0.1 collective-permute-start
  0.7 3.4 %collective-permute-start.1 = (bf16[576,128]{1,0:T(8,128)(2,1)}, bf16[576,128]{1,0:T(8,128)(2,1)S(1)}, u32[]{:S(2)}, u32[]{:S(2)}) collective-permute-start(bf16[576,128]{1,0:T(8,128)(2,1)} %bitcast.69), channel_id=1, source_target_pairs={{0,32},{32,64},{64,96},{1,33},{33,65},{65,97},{2,34},{34,66},{66,9... | collective-permute-start | bytes 442376 | tf_op jit(solution)/shard_map/ppermute | solution.py:287
  4.1 0.3 collective-permute-start.2
  4.4 2.9 %copy.23 = bf16[1,128,64,128]{3,1,2,0:T(8,128)(2,1)S(1)} copy(bf16[1,128,64,128]{3,2,1,0:T(8,128)(2,1)} %param.9) | data formatting | bytes 4194304 | tf_op args[4]
  7.4 0.0 copy-start.11
  7.4 0.0 copy-start.6
  7.4 0.8 collective-permute-done.1.prev_same
  8.2 0.0 collective-permute-done.2.mate
  8.2 1.1 constant_dynamic-slice_fusion
  9.3 0.0 collective-permute-start.3
  9.3 0.2 reduce-window.8
  9.4 0.1 select_reduce_fusion
  9.5 0.5 collective-permute-start.4
  10.1 0.1 pad_add_fusion.2.info
  10.1 2.1 %collective-permute-done.4.prev_mate = bf16[576,128]{1,0:T(8,128)(2,1)} collective-permute-done((bf16[576,128]{1,0:T(8,128)(2,1)S(1)}, bf16[576,128]{1,0:T(8,128)(2,1)}, u32[]{:S(2)}, u32[]{:S(2)}) %collective-permute-start.4) | collective-permute-done | bytes 147488 | tf_op jit(solution)/shard_map/ppermute | solution.py:295
  12.3 0.9 copy-done.8
  13.2 0.9 copy-done.10
  14.1 1.1 window.1
  15.3 20.2 %main_groups.3 = (bf16[64,192,128]{2,1,0:T(8,128)(2,1)}, bf16[32,192,128]{2,1,0:T(8,128)(2,1)}, bf16[4,4,512,128]{3,2,1,0:T(8,128)(2,1)}, bf16[4,4,512,128]{3,2,...) custom-call(s32[3]{0:T(128)S(1)} %pad_add_fusion.2.info, bf16[64,192,128]{2,1,0:T(8,128)(2,1)} %bitcast.76, ...), custom_call_target="tpu_custom_call" | custom-call | tf_op jit(solution)/shard_map/main_groups/pallas_call | solution.py:136
  35.5 2.4 %collective-permute-start.8 = (bf16[4,4,512,128]{3,2,1,0:T(8,128)(2,1)}, bf16[4,4,512,128]{3,2,1,0:T(8,128)(2,1)}, u32[]{:S(2)}, u32[]{:S(2)}) collective-permute-start(bf16[4,4,512,128]{3,2,1,0:T(8,128)(2,1)} %get-tuple-element.48), channel_id=1, source_target_pairs={{0,32},{32,64},{64,96},{96,0},{1,33},{33,65},{65,97},{97,1},{2,34}... | collective-permute-start | bytes 6291464 | tf_op jit(solution)/shard_map/ppermute | solution.py:308
  37.9 1.4 %collective-permute-start.9 = (bf16[4,4,512,128]{3,2,1,0:T(8,128)(2,1)}, bf16[4,4,512,128]{3,2,1,0:T(8,128)(2,1)}, u32[]{:S(2)}, u32[]{:S(2)}) collective-permute-start(bf16[4,4,512,128]{3,2,1,0:T(8,128)(2,1)} %get-tuple-element.49), channel_id=1, source_target_pairs={{0,96},{32,0},{64,32},{96,64},{1,97},{33,1},{65,33},{97,65},{2,98}... | collective-permute-start | bytes 6291464 | tf_op jit(solution)/shard_map/ppermute | solution.py:309
  39.3 0.1 pad_add_fusion
  39.4 1.0 copy-done.1
  40.4 1.0 copy-done.4
  41.5 11.5 %main_groups.4 = (bf16[64,192,128]{2,1,0:T(8,128)(2,1)}, bf16[32,192,128]{2,1,0:T(8,128)(2,1)}, bf16[4,4,512,128]{3,2,1,0:T(8,128)(2,1)}, f32[512,512]{1,0:T(8,128)}, f32[512,64]{1,0:T(8,128)}) custom-call(s32[2]{0:T(128)S(1)} %get-tuple-element.58.info, bf16[64,192,128]{2,1,0:T(8,128)(2,1)} %bitcast.77, ...), custom_call_target="tpu_custom_call", output_to_operand_aliasing={{0}: (10, {}), {1}: (11, {})} | custom-call | tf_op jit(solution)/shard_map/main_groups/pallas_call | solution.py:136
  53.0 8.4 %all-to-all-start.1 = ((bf16[16,512,128]{2,1,0:T(8,128)(2,1)}), bf16[16,512,128]{2,1,0:T(8,128)(2,1)}, u32[]{:S(2)}, u32[]{:S(2)}) async-start(bf16[16,512,128]{2,1,0:T(8,128)(2,1)} %bitcast.81), calls=%async_computation.1 | async-start | bytes 4194304 | tf_op jit(solution)/shard_map/all_to_all | solution.py:267
  61.4 1.0 copy-done.2
  62.4 1.0 copy-done.5
  63.5 11.5 %main_groups.5 = (bf16[64,192,128]{2,1,0:T(8,128)(2,1)}, bf16[32,192,128]{2,1,0:T(8,128)(2,1)}, bf16[4,4,512,128]{3,2,1,0:T(8,128)(2,1)}, f32[512,512]{1,0:T(8,128)}, f32[512,64]{1,0:T(8,128)}) custom-call(s32[2]{0:T(128)S(1)} %get-tuple-element.57.info, bf16[64,192,128]{2,1,0:T(8,128)(2,1)} %bitcast.78, ...), custom_call_target="tpu_custom_call", output_to_operand_aliasing={{0}: (10, {}), {1}: (11, {})} | custom-call | tf_op jit(solution)/shard_map/main_groups/pallas_call | solution.py:136
  75.0 10.5 %collective-permute-done.8 = bf16[4,4,512,128]{3,2,1,0:T(8,128)(2,1)} collective-permute-done((bf16[4,4,512,128]{3,2,1,0:T(8,128)(2,1)}, bf16[4,4,512,128]{3,2,1,0:T(8,128)(2,1)}, u32[]{:S(2)}, u32[]{:S(2)}) %collective-permute-start.8) | collective-permute-done | bytes 2097184 | tf_op jit(solution)/shard_map/ppermute | solution.py:308
  85.5 0.2 collective-permute-done.9
  85.6 5.1 %add_convert_fusion = bf16[4,4,512,128]{3,2,1,0:T(8,128)(2,1)} fusion(bf16[4,4,512,128]{3,2,1,0:T(8,128)(2,1)} %collective-permute-done.9, bf16[4,4,512,128]{3,2,1,0:T(8,128)(2,1)} %collective-permute-done.8, bf16[4,4,512,128]{3,2,1,0:T(8,128)(2,1)} %get-tuple-element.47), kind=kLoop, calls=%fused_computation.1 | loop fusion | flops 6291456 | bytes 8388608 | tf_op jit(solution)/shard_map/convert_element_type | solution.py:325
  90.7 8.4 %all-to-all-start = ((bf16[16,512,128]{2,1,0:T(8,128)(2,1)}), bf16[16,512,128]{2,1,0:T(8,128)(2,1)S(1)}, u32[]{:S(2)}, u32[]{:S(2)}) async-start(bf16[16,512,128]{2,1,0:T(8,128)(2,1)} %bitcast.80), calls=%async_computation | async-start | bytes 4194304 | tf_op jit(solution)/shard_map/all_to_all | solution.py:267
  99.2 4.3 %fold.1 = (f32[4,576,128]{2,1,0:T(8,128)}, bf16[4,576,128]{2,1,0:T(8,128)(2,1)}) custom-call(f32[512,512]{1,0:T(8,128)} %get-tuple-element.39.refs_0_, f32[512,64]{1,0:T(8,128)} %get-tuple-element.40.refs_1_, f32[512,512]{1,0:T(8,128)} %get-tuple-element.41.refs_2_, f32[512,64]{1,0:T(8,128)} %get-tuple-element.42.refs_3_, ...), custom_call_target="tpu_custom_call" | custom-call | tf_op jit(solution)/shard_map/fold/pallas_call | solution.py:170
  103.5 1.0 dynamic-slice_bitcast_fusion.2
  104.5 0.6 collective-permute-start.6
  105.0 1.2 collective-permute-done.6
  106.2 1.0 fusion.1
  107.2 1.3 collective-permute-start.7
  108.5 6.7 %collective-permute-done.7 = bf16[576,128]{1,0:T(8,128)(2,1)S(1)} collective-permute-done((bf16[576,128]{1,0:T(8,128)(2,1)S(1)}, bf16[576,128]{1,0:T(8,128)(2,1)S(1)}, u32[]{:S(2)}, u32[]{:S(2)}) %collective-permute-start.7) | collective-permute-done | bytes 147488 | tf_op jit(solution)/shard_map/ppermute | solution.py:327
  115.2 1.7 %fusion.5 = bf16[1,128,576]{1,2,0:T(8,128)(2,1)} fusion(bf16[576,128]{1,0:T(8,128)(2,1)S(1)} %collective-permute-done.7, f32[2,2,576,128]{3,2,1,0:T(8,128)} %bitcast.83, s32[]{:T(128)S(6)} %add.66, s32[]{:T(128)S(6)} %select_n.16, bf16[2,576,128]{2,1,0:T(8,128)(2,1)S(1)} %collective-permute-done.6), kind=kLoop, calls=%fused_computation.12 | loop fusion | flops 368640 | bytes 737288 | tf_op jit(solution)/shard_map/broadcast_in_dim | solution.py:331
  116.9 3.6 %place.1 = bf16[64,192,128]{2,1,0:T(8,128)(2,1)} custom-call(s32[1]{0:T(128)} %bitcast.info, bf16[32,192,128]{2,1,0:T(8,128)(2,1)} %collective-permute-done.5.got_ref, bf16[64,192,128]{2,1,0:T(8,128)(2,1)} %get-tuple-element.38.held_ref), custom_call_target="tpu_custom_call", output_to_operand_aliasing={{}: (2, {})} | custom-call | tf_op jit(solution)/shard_map/place/pallas_call | solution.py:229
  120.5 1.9 %reduce_sum.32 = bf16[512,128]{1,0:T(8,128)(2,1)S(1)} reduce(bf16[16,512,128]{2,1,0:T(8,128)(2,1)} %all-to-all-done.1, bf16[]{:T(256)} %constant.52.clone.1), dimensions={0}, to_apply=%region_3.4 | reduce | flops 983040 | bytes 2228226 | tf_op jit(solution)/shard_map/reduce_sum | solution.py:271
  122.4 2.8 %collective-permute-start.10 = (bf16[512,128]{1,0:T(8,128)(2,1)S(1)}, bf16[512,128]{1,0:T(8,128)(2,1)S(1)}, u32[]{:S(2)}, u32[]{:S(2)}) collective-permute-start(bf16[512,128]{1,0:T(8,128)(2,1)S(1)} %reduce_sum.32), channel_id=1, source_target_pairs={{0,64},{32,96},{64,0},{96,32},{1,65},{33,97},{65,1},{97,33},{2,66}... | collective-permute-start | bytes 393224 | tf_op jit(solution)/shard_map/ppermute | solution.py:324
  125.2 0.7 all-to-all-done
  125.9 0.3 convert_reduce_fusion
  126.2 2.7 %collective-permute-done.10 = bf16[512,128]{1,0:T(8,128)(2,1)S(1)} collective-permute-done((bf16[512,128]{1,0:T(8,128)(2,1)S(1)}, bf16[512,128]{1,0:T(8,128)(2,1)S(1)}, u32[]{:S(2)}, u32[]{:S(2)}) %collective-permute-start.10) | collective-permute-done | bytes 131104 | tf_op jit(solution)/shard_map/ppermute | solution.py:324
  129.0 0.8 copy.20
  (24 shorter events, 0.1 us)
Async XLA Ops:
  0.6 14.6 %collective-permute-start = (bf16[64,192,128]{2,1,0:T(8,128)(2,1)}, bf16[64,192,128]{2,1,0:T(8,128)(2,1)}, u32[]{:S(2)}, u32[]{:S(2)}) collective-permute-start(bf16[64,192,128]{2,1,0:T(8,128)(2,1)} %bitcast.75), channel_id=1, source_target_pairs={{0,16},{16,0},{1,17},{17,1},{2,18},{18,2},{3,19},{19,3},{4,20},{20... | collective-permute-start | bytes 9437192 | tf_op jit(solution)/shard_map/ppermute | solution.py:289
  0.7 7.5 %collective-permute-start.1 = (bf16[576,128]{1,0:T(8,128)(2,1)}, bf16[576,128]{1,0:T(8,128)(2,1)S(1)}, u32[]{:S(2)}, u32[]{:S(2)}) collective-permute-start(bf16[576,128]{1,0:T(8,128)(2,1)} %bitcast.69), channel_id=1, source_target_pairs={{0,32},{32,64},{64,96},{1,33},{33,65},{65,97},{2,34},{34,66},{66,9... | collective-permute-start | bytes 442376 | tf_op jit(solution)/shard_map/ppermute | solution.py:287
  4.1 4.0 %collective-permute-start.2 = (bf16[576,128]{1,0:T(8,128)(2,1)}, bf16[576,128]{1,0:T(8,128)(2,1)S(1)}, u32[]{:S(2)}, u32[]{:S(2)}) collective-permute-start(bf16[576,128]{1,0:T(8,128)(2,1)} %bitcast.70), channel_id=1, source_target_pairs={{0,16},{16,0},{1,17},{17,1},{2,18},{18,2},{3,19},{19,3},{4,20},{20... | collective-permute-start | bytes 442376 | tf_op jit(solution)/shard_map/ppermute | solution.py:286
  7.4 1.9 %copy-start.11 = (s32[1,8]{1,0:T(1,128)S(1)}, s32[1,8]{1,0:T(1,128)}, u32[]{:S(2)}) copy-start(s32[1,8]{1,0:T(1,128)} %param.7) | copy-start | bytes 100
  7.4 4.9 %copy-start.6 = (bf16[1,128,576]{1,2,0:T(8,128)(2,1)S(1)}, bf16[1,128,576]{1,2,0:T(8,128)(2,1)}, u32[]{:S(2)}) copy-start(bf16[1,128,576]{1,2,0:T(8,128)(2,1)} %param.6) | copy-start | bytes 442372
  8.2 1.9 %copy-start.7 = (bf16[576,128]{1,0:T(8,128)(2,1)}, bf16[576,128]{1,0:T(8,128)(2,1)S(1)}, u32[]{:S(2)}) copy-start(bf16[576,128]{1,0:T(8,128)(2,1)S(1)} %collective-permute-done.1.prev_same) | copy-start | bytes 442372
  8.2 1.1 copy-start.9
  9.3 6.0 %collective-permute-start.3 = (bf16[32,128,128]{2,1,0:T(8,128)(2,1)}, bf16[32,128,128]{2,1,0:T(8,128)(2,1)S(1)}, u32[]{:S(2)}, u32[]{:S(2)}) collective-permute-start(bf16[32,128,128]{2,1,0:T(8,128)(2,1)} %bitcast.11), channel_id=1, source_target_pairs={{0,16},{16,0},{1,17},{17,1},{2,18},{18,2},{3,19},{19,3},{4,20},{20... | collective-permute-start | bytes 3145736 | tf_op jit(solution)/shard_map/ppermute | solution.py:292
  9.5 2.7 %collective-permute-start.4 = (bf16[576,128]{1,0:T(8,128)(2,1)S(1)}, bf16[576,128]{1,0:T(8,128)(2,1)}, u32[]{:S(2)}, u32[]{:S(2)}) collective-permute-start(bf16[576,128]{1,0:T(8,128)(2,1)S(1)} %collective-permute-done.1.prev_same), channel_id=1, source_target_pairs={{0,16},{16,0},{1,17},{17,1},{2,18},{18,2},{3,19},{19,3},{4,20},{20... | collective-permute-start | bytes 442376 | tf_op jit(solution)/shard_map/ppermute | solution.py:295
  12.3 0.9 copy-start.8
  13.2 0.9 copy-start.10
  15.2 20.2 %copy-start = (bf16[512,512]{1,0:T(8,128)(2,1)}, bf16[512,512]{1,0:T(8,128)(2,1)S(1)}, u32[]{:S(2)}) copy-start(bf16[512,512]{1,0:T(8,128)(2,1)S(1)} %get-tuple-element.30.refs_5_) | copy-start | bytes 1572868
  15.2 20.2 %copy-start.3 = (bf16[512,512]{1,0:T(8,128)(2,1)}, bf16[512,512]{1,0:T(8,128)(2,1)S(1)}, u32[]{:S(2)}) copy-start(bf16[512,512]{1,0:T(8,128)(2,1)S(1)} %get-tuple-element.31.refs_6_) | copy-start | bytes 1572868
  35.5 50.0 %collective-permute-start.8 = (bf16[4,4,512,128]{3,2,1,0:T(8,128)(2,1)}, bf16[4,4,512,128]{3,2,1,0:T(8,128)(2,1)}, u32[]{:S(2)}, u32[]{:S(2)}) collective-permute-start(bf16[4,4,512,128]{3,2,1,0:T(8,128)(2,1)} %get-tuple-element.48), channel_id=1, source_target_pairs={{0,32},{32,64},{64,96},{96,0},{1,33},{33,65},{65,97},{97,1},{2,34}... | collective-permute-start | bytes 6291464 | tf_op jit(solution)/shard_map/ppermute | solution.py:308
  37.9 47.7 %collective-permute-start.9 = (bf16[4,4,512,128]{3,2,1,0:T(8,128)(2,1)}, bf16[4,4,512,128]{3,2,1,0:T(8,128)(2,1)}, u32[]{:S(2)}, u32[]{:S(2)}) collective-permute-start(bf16[4,4,512,128]{3,2,1,0:T(8,128)(2,1)} %get-tuple-element.49), channel_id=1, source_target_pairs={{0,96},{32,0},{64,32},{96,64},{1,97},{33,1},{65,33},{97,65},{2,98}... | collective-permute-start | bytes 6291464 | tf_op jit(solution)/shard_map/ppermute | solution.py:309
  39.4 1.0 copy-start.1
  40.4 1.0 copy-start.4
  53.0 37.8 %all-to-all-start.1 = ((bf16[16,512,128]{2,1,0:T(8,128)(2,1)}), bf16[16,512,128]{2,1,0:T(8,128)(2,1)}, u32[]{:S(2)}, u32[]{:S(2)}) async-start(bf16[16,512,128]{2,1,0:T(8,128)(2,1)} %bitcast.81), calls=%async_computation.1 | async-start | bytes 4194304 | tf_op jit(solution)/shard_map/all_to_all | solution.py:267
  61.4 1.0 copy-start.2
  62.4 1.0 copy-start.5
  90.7 35.2 %all-to-all-start = ((bf16[16,512,128]{2,1,0:T(8,128)(2,1)}), bf16[16,512,128]{2,1,0:T(8,128)(2,1)S(1)}, u32[]{:S(2)}, u32[]{:S(2)}) async-start(bf16[16,512,128]{2,1,0:T(8,128)(2,1)} %bitcast.80), calls=%async_computation | async-start | bytes 4194304 | tf_op jit(solution)/shard_map/all_to_all | solution.py:267
  99.2 17.8 %collective-permute-start.5 = (bf16[32,192,128]{2,1,0:T(8,128)(2,1)}, bf16[32,192,128]{2,1,0:T(8,128)(2,1)}, u32[]{:S(2)}, u32[]{:S(2)}) collective-permute-start(bf16[32,192,128]{2,1,0:T(8,128)(2,1)} %get-tuple-element.37), channel_id=1, source_target_pairs={{0,16},{16,0},{1,17},{17,1},{2,18},{18,2},{3,19},{19,3},{4,20},{20... | collective-permute-start | bytes 4718600 | tf_op jit(solution)/shard_map/ppermute | solution.py:314
  104.5 1.8 %collective-permute-start.6 = (bf16[2,576,128]{2,1,0:T(8,128)(2,1)S(1)}, bf16[2,576,128]{2,1,0:T(8,128)(2,1)S(1)}, u32[]{:S(2)}, u32[]{:S(2)}) collective-permute-start(bf16[2,576,128]{2,1,0:T(8,128)(2,1)S(1)} %dynamic-slice_bitcast_fusion.2), channel_id=1, source_target_pairs={{0,16},{16,0},{1,17},{17,1},{2,18},{18,2},{3,19},{19,3},{4,20},{20... | collective-permute-start | bytes 884744 | tf_op jit(solution)/shard_map/ppermute | solution.py:320
  107.2 8.0 %collective-permute-start.7 = (bf16[576,128]{1,0:T(8,128)(2,1)S(1)}, bf16[576,128]{1,0:T(8,128)(2,1)S(1)}, u32[]{:S(2)}, u32[]{:S(2)}) collective-permute-start(bf16[576,128]{1,0:T(8,128)(2,1)S(1)} %fusion.1), channel_id=1, source_target_pairs={{32,0},{64,32},{96,64},{33,1},{65,33},{97,65},{34,2},{66,34},{98,6... | collective-permute-start | bytes 442376 | tf_op jit(solution)/shard_map/ppermute | solution.py:327
  122.4 6.6 %collective-permute-start.10 = (bf16[512,128]{1,0:T(8,128)(2,1)S(1)}, bf16[512,128]{1,0:T(8,128)(2,1)S(1)}, u32[]{:S(2)}, u32[]{:S(2)}) collective-permute-start(bf16[512,128]{1,0:T(8,128)(2,1)S(1)} %reduce_sum.32), channel_id=1, source_target_pairs={{0,64},{32,96},{64,0},{96,32},{1,65},{33,97},{65,1},{97,33},{2,66}... | collective-permute-start | bytes 393224 | tf_op jit(solution)/shard_map/ppermute | solution.py:324

commit v3 on v2

--- a/solution.py
+++ b/solution.py
@@ -29,6 +29,10 @@
 LOG2E = math.log2(math.e)
 NT = (((1,), (1,)), ((), ()))
 TN = (((0,), (0,)), ((), ()))
+
+
+def in_hbm(array):
+    return pltpu.with_memory_space_constraint(array, pltpu.HBM)
 
 
 def mm(a, b, dims=(((1,), (0,)), ((), ()))):
@@ -150,7 +154,7 @@
             flops=0, bytes_accessed=0, transcendentals=0
         ),
         name="main_groups",
-    )(info, q_full, q_got, g_full, g_got, w_kv, lat, latt, rope, low, *held)
+    )(info, q_full, q_got, g_full, g_got, w_kv, in_hbm(lat), in_hbm(latt), rope, low, *held)
     return tuple(outs[:2]), outs[2 : 2 + groups], (outs[-2], outs[-1])
 
 
@@ -197,18 +201,31 @@
 
 
 def window_of(info, pieces):
+    whole = lambda i, info: (0, 0)
+    grid_spec = pltpu.PrefetchScalarGridSpec(
+        num_scalar_prefetch=1,
+        grid=(1,),
+        in_specs=[pl.BlockSpec((LAT + ROPE, ROWS), whole)] * 4,
+        out_specs=[
+            pl.BlockSpec((KEYS, LAT), whole),
+            pl.BlockSpec((LAT, KEYS), whole),
+            pl.BlockSpec((KEYS, ROPE), whole),
+        ],
+    )
     return pl.pallas_call(
         window_kernel,
-        in_specs=[pl.BlockSpec(memory_space=pltpu.SMEM)]
-        + [pl.BlockSpec(memory_space=pltpu.VMEM)] * 4,
+        grid_spec=grid_spec,
         out_shape=[
-            jax.ShapeDtypeStruct((KEYS, LAT), BF16),
-            jax.ShapeDtypeStruct((LAT, KEYS), BF16),
+            pltpu.HBM((KEYS, LAT), BF16),
+            pltpu.HBM((LAT, KEYS), BF16),
             jax.ShapeDtypeStruct((KEYS, ROPE), BF16),
         ],
-        compiler_params=pltpu.CompilerParams(vmem_limit_bytes=32 * 1024 * 1024),
+        compiler_params=pltpu.CompilerParams(
+            dimension_semantics=("arbitrary",), vmem_limit_bytes=32 * 1024 * 1024
+        ),
+        cost_estimate=pl.CostEstimate(flops=0, bytes_accessed=0, transcendentals=0),
         name="window",
-    )(info, *pieces)
+    )(info, *[in_hbm(piece) for piece in pieces])
 
 
 def place_kernel(info, got_ref, held_ref, out_ref):

time: 131 us -> 130 us (level)
  local copies, waits for them, and re-layouts: 11.8 us -> 5.83 us
  waiting for transfers between devices: 25 us -> 28.5 us
  Pallas kernels: 52.2 us -> 54.5 us
    unnamed x26 -> x8, local copies, waits for them, and re-layouts: 9.79 us -> 3.79 us
    ppermute x1, waiting for transfers between devices: 10.5 us -> 13.9 us  [per_device(): from_left = lax.ppermute(dw_left, 'x', ring(1))]
  transfers between devices with their start and end apart: 13 -> 13, of which waited for: 8 -> 8; matrix products, arithmetic and copies ran while one was open for 12% -> 12% of each run, Pallas kernels for 25% -> 26%
where the time goes in v3:
time: 130 us
  Pallas kernels  54.5 us (42%)
  starting transfers between devices  29.6 us (23%)
  waiting for transfers between devices  28.5 us (22%)
  other arithmetic  10.4 us (8%)
  local copies, waits for them, and re-layouts  5.83 us (4%)
    pallas_call x3, Pallas kernels, main_groups(): pl.pallas_call(functools.partial(main_kernel, groups), grid_spec=grid_spe...  44.5 us
    all_to_all x2, starting transfers between devices, all_to_all(): return lax.all_to_all(blocks, axis, 0, 0, tiled=True)  16.8 us
    ppermute x1, waiting for transfers between devices, per_device(): from_left = lax.ppermute(dw_left, 'x', ring(1))  13.9 us
    ppermute x1, waiting for transfers between devices, per_device(): from_next = lax.ppermute(prev_sum, 'x', [(i + 1, i) for i in range(NX - 1)])  6.72 us
    convert_element_type x1, other arithmetic, per_device(): mine = total([dw_own, from_left, from_right]).astype(BF16)  5.09 us
    pallas_call x1, Pallas kernels, fold(): pl.pallas_call(fold_kernel, grid=(KEYS // ROWS,), in_specs=[pl.BlockSpec(...  4.3 us
    unnamed x8, local copies, waits for them, and re-layouts  3.79 us
    pallas_call x1, Pallas kernels, place(): pl.pallas_call(place_kernel, grid_spec=grid_spec, out_shape=pltpu.HBM((HE...  3.56 us
  transfers between devices with their start and end apart: 13, of which 8 were waited for; matrix products, arithmetic and copies ran while one was open for 12% of the time, Pallas kernels for 26%

profile of v3, /device:TPU:8, one launch (start us, length us, event | category | flops | bytes accessed | tf_op | source)
XLA Modules:
  0.0 129.5 jit_solution(9531205024418407951)
XLA Ops:
  0.6 0.1 collective-permute-start
  0.7 3.4 %collective-permute-start.1 = (bf16[576,128]{1,0:T(8,128)(2,1)}, bf16[576,128]{1,0:T(8,128)(2,1)S(1)}, u32[]{:S(2)}, u32[]{:S(2)}) collective-permute-start(bf16[576,128]{1,0:T(8,128)(2,1)} %bitcast.82), channel_id=1, source_target_pairs={{0,32},{32,64},{64,96},{1,33},{33,65},{65,97},{2,34},{34,66},{66,9... | collective-permute-start | bytes 442376 | tf_op jit(solution)/shard_map/ppermute | solution.py:304
  4.1 0.3 collective-permute-start.2
  4.4 2.9 %copy.23 = bf16[1,128,64,128]{3,1,2,0:T(8,128)(2,1)S(1)} copy(bf16[1,128,64,128]{3,2,1,0:T(8,128)(2,1)} %param.9) | data formatting | bytes 4194304 | tf_op args[4]
  7.4 0.0 copy-start.2
  7.4 0.8 collective-permute-done.1.prev_same
  8.2 0.0 collective-permute-done.2.mate
  8.2 1.1 constant_dynamic-slice_fusion
  9.2 0.0 copy-done.1
  9.3 0.0 collective-permute-start.3
  9.3 0.0 copy-done.2
  9.3 0.2 reduce-window.8
  9.4 0.1 select_reduce_fusion
  9.5 0.5 collective-permute-start.4
  10.1 0.1 pad_add_fusion.2.info
  10.1 2.1 %collective-permute-done.4.prev_mate = bf16[576,128]{1,0:T(8,128)(2,1)} collective-permute-done((bf16[576,128]{1,0:T(8,128)(2,1)S(1)}, bf16[576,128]{1,0:T(8,128)(2,1)}, u32[]{:S(2)}, u32[]{:S(2)}) %collective-permute-start.4) | collective-permute-done | bytes 147488 | tf_op jit(solution)/shard_map/ppermute | solution.py:312
  12.3 2.2 %window.1 = (bf16[512,512]{1,0:T(8,128)(2,1)}, bf16[512,512]{1,0:T(8,128)(2,1)}, bf16[512,64]{1,0:T(8,128)(2,1)S(1)}) custom-call(s32[1]{0:T(128)} %bitcast.info, bf16[576,128]{1,0:T(8,128)(2,1)} %bitcast.84, bf16[576,128]{1,0:T(8,128)(2,1)} %copy-done.1, bf16[576,128]{1,0:T(8,128)(2,1)} %copy-done, bf16[576,128]{1,0:T(8,128)(2,1)} %collective-permute-done.4.prev_mate), custom_call_target="tpu_custom_call" | custom-call | tf_op jit(solution)/shard_map/window/pallas_call | solution.py:215
  14.4 0.0 collective-permute-done.3.refs_3_
  14.4 0.0 collective-permute-done.refs_1_
  14.4 20.8 %main_groups.3 = (bf16[64,192,128]{2,1,0:T(8,128)(2,1)}, bf16[32,192,128]{2,1,0:T(8,128)(2,1)}, bf16[4,4,512,128]{3,2,1,0:T(8,128)(2,1)}, bf16[4,4,512,128]{3,2,...) custom-call(s32[3]{0:T(128)S(1)} %pad_add_fusion.2.info, bf16[64,192,128]{2,1,0:T(8,128)(2,1)} %bitcast.73, ...), custom_call_target="tpu_custom_call" | custom-call | tf_op jit(solution)/shard_map/main_groups/pallas_call | solution.py:140
  35.2 2.4 %collective-permute-start.8 = (bf16[4,4,512,128]{3,2,1,0:T(8,128)(2,1)}, bf16[4,4,512,128]{3,2,1,0:T(8,128)(2,1)}, u32[]{:S(2)}, u32[]{:S(2)}) collective-permute-start(bf16[4,4,512,128]{3,2,1,0:T(8,128)(2,1)} %get-tuple-element.48), channel_id=1, source_target_pairs={{0,32},{32,64},{64,96},{96,0},{1,33},{33,65},{65,97},{97,1},{2,34}... | collective-permute-start | bytes 6291464 | tf_op jit(solution)/shard_map/ppermute | solution.py:325
  37.7 1.4 %collective-permute-start.9 = (bf16[4,4,512,128]{3,2,1,0:T(8,128)(2,1)}, bf16[4,4,512,128]{3,2,1,0:T(8,128)(2,1)}, u32[]{:S(2)}, u32[]{:S(2)}) collective-permute-start(bf16[4,4,512,128]{3,2,1,0:T(8,128)(2,1)} %get-tuple-element.49), channel_id=1, source_target_pairs={{0,96},{32,0},{64,32},{96,64},{1,97},{33,1},{65,33},{97,65},{2,98}... | collective-permute-start | bytes 6291464 | tf_op jit(solution)/shard_map/ppermute | solution.py:326
  39.0 0.1 pad_add_fusion
  39.1 11.8 %main_groups.4 = (bf16[64,192,128]{2,1,0:T(8,128)(2,1)}, bf16[32,192,128]{2,1,0:T(8,128)(2,1)}, bf16[4,4,512,128]{3,2,1,0:T(8,128)(2,1)}, f32[512,512]{1,0:T(8,128)}, f32[512,64]{1,0:T(8,128)}) custom-call(s32[2]{0:T(128)S(1)} %get-tuple-element.58.info, bf16[64,192,128]{2,1,0:T(8,128)(2,1)} %bitcast.74, ...), custom_call_target="tpu_custom_call", output_to_operand_aliasing={{0}: (10, {}), {1}: (11, {})} | custom-call | tf_op jit(solution)/shard_map/main_groups/pallas_call | solution.py:140
  50.9 8.4 %all-to-all-start.1 = ((bf16[16,512,128]{2,1,0:T(8,128)(2,1)}), bf16[16,512,128]{2,1,0:T(8,128)(2,1)}, u32[]{:S(2)}, u32[]{:S(2)}) async-start(bf16[16,512,128]{2,1,0:T(8,128)(2,1)} %bitcast.78), calls=%async_computation.1 | async-start | bytes 4194304 | tf_op jit(solution)/shard_map/all_to_all | solution.py:284
  59.4 11.9 %main_groups.5 = (bf16[64,192,128]{2,1,0:T(8,128)(2,1)}, bf16[32,192,128]{2,1,0:T(8,128)(2,1)}, bf16[4,4,512,128]{3,2,1,0:T(8,128)(2,1)}, f32[512,512]{1,0:T(8,128)}, f32[512,64]{1,0:T(8,128)}) custom-call(s32[2]{0:T(128)S(1)} %get-tuple-element.57.info, bf16[64,192,128]{2,1,0:T(8,128)(2,1)} %bitcast.75, ...), custom_call_target="tpu_custom_call", output_to_operand_aliasing={{0}: (10, {}), {1}: (11, {})} | custom-call | tf_op jit(solution)/shard_map/main_groups/pallas_call | solution.py:140
  71.2 13.9 %collective-permute-done.8 = bf16[4,4,512,128]{3,2,1,0:T(8,128)(2,1)} collective-permute-done((bf16[4,4,512,128]{3,2,1,0:T(8,128)(2,1)}, bf16[4,4,512,128]{3,2,1,0:T(8,128)(2,1)}, u32[]{:S(2)}, u32[]{:S(2)}) %collective-permute-start.8) | collective-permute-done | bytes 2097184 | tf_op jit(solution)/shard_map/ppermute | solution.py:325
  85.2 0.2 collective-permute-done.9
  85.4 5.1 %add_convert_fusion = bf16[4,4,512,128]{3,2,1,0:T(8,128)(2,1)} fusion(bf16[4,4,512,128]{3,2,1,0:T(8,128)(2,1)} %collective-permute-done.9, bf16[4,4,512,128]{3,2,1,0:T(8,128)(2,1)} %collective-permute-done.8, bf16[4,4,512,128]{3,2,1,0:T(8,128)(2,1)} %get-tuple-element.47), kind=kLoop, calls=%fused_computation.1 | loop fusion | flops 6291456 | bytes 8388608 | tf_op jit(solution)/shard_map/convert_element_type | solution.py:342
  90.5 0.0 all-to-all-done.1
  90.5 8.4 %all-to-all-start = ((bf16[16,512,128]{2,1,0:T(8,128)(2,1)}), bf16[16,512,128]{2,1,0:T(8,128)(2,1)S(1)}, u32[]{:S(2)}, u32[]{:S(2)}) async-start(bf16[16,512,128]{2,1,0:T(8,128)(2,1)} %bitcast.77), calls=%async_computation | async-start | bytes 4194304 | tf_op jit(solution)/shard_map/all_to_all | solution.py:284
  98.9 0.0 collective-permute-start.5
  98.9 4.3 %fold.1 = (f32[4,576,128]{2,1,0:T(8,128)}, bf16[4,576,128]{2,1,0:T(8,128)(2,1)}) custom-call(f32[512,512]{1,0:T(8,128)} %get-tuple-element.39.refs_0_, f32[512,64]{1,0:T(8,128)} %get-tuple-element.40.refs_1_, f32[512,512]{1,0:T(8,128)} %get-tuple-element.41.refs_2_, f32[512,64]{1,0:T(8,128)} %get-tuple-element.42.refs_3_, ...), custom_call_target="tpu_custom_call" | custom-call | tf_op jit(solution)/shard_map/fold/pallas_call | solution.py:174
  103.2 1.0 dynamic-slice_bitcast_fusion.2
  104.2 0.6 collective-permute-start.6
  104.7 1.2 collective-permute-done.6
  105.9 1.0 fusion.1
  106.9 1.3 collective-permute-start.7
  108.2 6.7 %collective-permute-done.7 = bf16[576,128]{1,0:T(8,128)(2,1)S(1)} collective-permute-done((bf16[576,128]{1,0:T(8,128)(2,1)S(1)}, bf16[576,128]{1,0:T(8,128)(2,1)S(1)}, u32[]{:S(2)}, u32[]{:S(2)}) %collective-permute-start.7) | collective-permute-done | bytes 147488 | tf_op jit(solution)/shard_map/ppermute | solution.py:344
  115.0 1.7 %fusion.5 = bf16[1,128,576]{1,2,0:T(8,128)(2,1)} fusion(bf16[576,128]{1,0:T(8,128)(2,1)S(1)} %collective-permute-done.7, f32[2,2,576,128]{3,2,1,0:T(8,128)} %bitcast.80, s32[]{:T(128)S(6)} %add.66, s32[]{:T(128)S(6)} %select_n.16, bf16[2,576,128]{2,1,0:T(8,128)(2,1)S(1)} %collective-permute-done.6), kind=kLoop, calls=%fused_computation.12 | loop fusion | flops 368640 | bytes 737288 | tf_op jit(solution)/shard_map/broadcast_in_dim | solution.py:348
  116.6 0.0 collective-permute-done.5.got_ref
  116.6 3.6 %place.1 = bf16[64,192,128]{2,1,0:T(8,128)(2,1)} custom-call(s32[1]{0:T(128)} %bitcast.info, bf16[32,192,128]{2,1,0:T(8,128)(2,1)} %collective-permute-done.5.got_ref, bf16[64,192,128]{2,1,0:T(8,128)(2,1)} %get-tuple-element.38.held_ref), custom_call_target="tpu_custom_call", output_to_operand_aliasing={{}: (2, {})} | custom-call | tf_op jit(solution)/shard_map/place/pallas_call | solution.py:246
  120.2 1.9 %reduce_sum.32 = bf16[512,128]{1,0:T(8,128)(2,1)S(1)} reduce(bf16[16,512,128]{2,1,0:T(8,128)(2,1)} %all-to-all-done.1, bf16[]{:T(256)} %constant.52.clone.1), dimensions={0}, to_apply=%region_3.4 | reduce | flops 983040 | bytes 2228226 | tf_op jit(solution)/shard_map/reduce_sum | solution.py:288
  122.1 2.8 %collective-permute-start.10 = (bf16[512,128]{1,0:T(8,128)(2,1)S(1)}, bf16[512,128]{1,0:T(8,128)(2,1)S(1)}, u32[]{:S(2)}, u32[]{:S(2)}) collective-permute-start(bf16[512,128]{1,0:T(8,128)(2,1)S(1)} %reduce_sum.32), channel_id=1, source_target_pairs={{0,64},{32,96},{64,0},{96,32},{1,65},{33,97},{65,1},{97,33},{2,66}... | collective-permute-start | bytes 393224 | tf_op jit(solution)/shard_map/ppermute | solution.py:341
  124.9 0.7 all-to-all-done
  125.6 0.3 convert_reduce_fusion
  125.9 2.7 %collective-permute-done.10 = bf16[512,128]{1,0:T(8,128)(2,1)S(1)} collective-permute-done((bf16[512,128]{1,0:T(8,128)(2,1)S(1)}, bf16[512,128]{1,0:T(8,128)(2,1)S(1)}, u32[]{:S(2)}, u32[]{:S(2)}) %collective-permute-start.10) | collective-permute-done | bytes 131104 | tf_op jit(solution)/shard_map/ppermute | solution.py:341
  128.7 0.8 copy.20
  (6 shorter events, 0.0 us)
Async XLA Ops:
  0.6 13.8 %collective-permute-start = (bf16[64,192,128]{2,1,0:T(8,128)(2,1)}, bf16[64,192,128]{2,1,0:T(8,128)(2,1)}, u32[]{:S(2)}, u32[]{:S(2)}) collective-permute-start(bf16[64,192,128]{2,1,0:T(8,128)(2,1)} %bitcast.72), channel_id=1, source_target_pairs={{0,16},{16,0},{1,17},{17,1},{2,18},{18,2},{3,19},{19,3},{4,20},{20... | collective-permute-start | bytes 9437192 | tf_op jit(solution)/shard_map/ppermute | solution.py:306
  0.7 7.5 %collective-permute-start.1 = (bf16[576,128]{1,0:T(8,128)(2,1)}, bf16[576,128]{1,0:T(8,128)(2,1)S(1)}, u32[]{:S(2)}, u32[]{:S(2)}) collective-permute-start(bf16[576,128]{1,0:T(8,128)(2,1)} %bitcast.82), channel_id=1, source_target_pairs={{0,32},{32,64},{64,96},{1,33},{33,65},{65,97},{2,34},{34,66},{66,9... | collective-permute-start | bytes 442376 | tf_op jit(solution)/shard_map/ppermute | solution.py:304
  4.1 4.0 %collective-permute-start.2 = (bf16[576,128]{1,0:T(8,128)(2,1)}, bf16[576,128]{1,0:T(8,128)(2,1)S(1)}, u32[]{:S(2)}, u32[]{:S(2)}) collective-permute-start(bf16[576,128]{1,0:T(8,128)(2,1)} %bitcast.83), channel_id=1, source_target_pairs={{0,16},{16,0},{1,17},{17,1},{2,18},{18,2},{3,19},{19,3},{4,20},{20... | collective-permute-start | bytes 442376 | tf_op jit(solution)/shard_map/ppermute | solution.py:303
  7.4 1.9 %copy-start.2 = (s32[1,8]{1,0:T(1,128)S(1)}, s32[1,8]{1,0:T(1,128)}, u32[]{:S(2)}) copy-start(s32[1,8]{1,0:T(1,128)} %param.7) | copy-start | bytes 100
  8.2 4.1 %copy-start = (bf16[576,128]{1,0:T(8,128)(2,1)}, bf16[576,128]{1,0:T(8,128)(2,1)S(1)}, u32[]{:S(2)}) copy-start(bf16[576,128]{1,0:T(8,128)(2,1)S(1)} %collective-permute-done.1.prev_same) | copy-start | bytes 442372
  8.2 1.1 copy-start.1
  9.3 5.2 %collective-permute-start.3 = (bf16[32,128,128]{2,1,0:T(8,128)(2,1)}, bf16[32,128,128]{2,1,0:T(8,128)(2,1)S(1)}, u32[]{:S(2)}, u32[]{:S(2)}) collective-permute-start(bf16[32,128,128]{2,1,0:T(8,128)(2,1)} %bitcast.11), channel_id=1, source_target_pairs={{0,16},{16,0},{1,17},{17,1},{2,18},{18,2},{3,19},{19,3},{4,20},{20... | collective-permute-start | bytes 3145736 | tf_op jit(solution)/shard_map/ppermute | solution.py:309
  9.5 2.7 %collective-permute-start.4 = (bf16[576,128]{1,0:T(8,128)(2,1)S(1)}, bf16[576,128]{1,0:T(8,128)(2,1)}, u32[]{:S(2)}, u32[]{:S(2)}) collective-permute-start(bf16[576,128]{1,0:T(8,128)(2,1)S(1)} %collective-permute-done.1.prev_same), channel_id=1, source_target_pairs={{0,16},{16,0},{1,17},{17,1},{2,18},{18,2},{3,19},{19,3},{4,20},{20... | collective-permute-start | bytes 442376 | tf_op jit(solution)/shard_map/ppermute | solution.py:312
  35.2 50.0 %collective-permute-start.8 = (bf16[4,4,512,128]{3,2,1,0:T(8,128)(2,1)}, bf16[4,4,512,128]{3,2,1,0:T(8,128)(2,1)}, u32[]{:S(2)}, u32[]{:S(2)}) collective-permute-start(bf16[4,4,512,128]{3,2,1,0:T(8,128)(2,1)} %get-tuple-element.48), channel_id=1, source_target_pairs={{0,32},{32,64},{64,96},{96,0},{1,33},{33,65},{65,97},{97,1},{2,34}... | collective-permute-start | bytes 6291464 | tf_op jit(solution)/shard_map/ppermute | solution.py:325
  37.7 47.7 %collective-permute-start.9 = (bf16[4,4,512,128]{3,2,1,0:T(8,128)(2,1)}, bf16[4,4,512,128]{3,2,1,0:T(8,128)(2,1)}, u32[]{:S(2)}, u32[]{:S(2)}) collective-permute-start(bf16[4,4,512,128]{3,2,1,0:T(8,128)(2,1)} %get-tuple-element.49), channel_id=1, source_target_pairs={{0,96},{32,0},{64,32},{96,64},{1,97},{33,1},{65,33},{97,65},{2,98}... | collective-permute-start | bytes 6291464 | tf_op jit(solution)/shard_map/ppermute | solution.py:326
  50.9 39.5 %all-to-all-start.1 = ((bf16[16,512,128]{2,1,0:T(8,128)(2,1)}), bf16[16,512,128]{2,1,0:T(8,128)(2,1)}, u32[]{:S(2)}, u32[]{:S(2)}) async-start(bf16[16,512,128]{2,1,0:T(8,128)(2,1)} %bitcast.78), calls=%async_computation.1 | async-start | bytes 4194304 | tf_op jit(solution)/shard_map/all_to_all | solution.py:284
  90.5 35.2 %all-to-all-start = ((bf16[16,512,128]{2,1,0:T(8,128)(2,1)}), bf16[16,512,128]{2,1,0:T(8,128)(2,1)S(1)}, u32[]{:S(2)}, u32[]{:S(2)}) async-start(bf16[16,512,128]{2,1,0:T(8,128)(2,1)} %bitcast.77), calls=%async_computation | async-start | bytes 4194304 | tf_op jit(solution)/shard_map/all_to_all | solution.py:284
  98.9 17.8 %collective-permute-start.5 = (bf16[32,192,128]{2,1,0:T(8,128)(2,1)}, bf16[32,192,128]{2,1,0:T(8,128)(2,1)}, u32[]{:S(2)}, u32[]{:S(2)}) collective-permute-start(bf16[32,192,128]{2,1,0:T(8,128)(2,1)} %get-tuple-element.37), channel_id=1, source_target_pairs={{0,16},{16,0},{1,17},{17,1},{2,18},{18,2},{3,19},{19,3},{4,20},{20... | collective-permute-start | bytes 4718600 | tf_op jit(solution)/shard_map/ppermute | solution.py:331
  104.2 1.8 %collective-permute-start.6 = (bf16[2,576,128]{2,1,0:T(8,128)(2,1)S(1)}, bf16[2,576,128]{2,1,0:T(8,128)(2,1)S(1)}, u32[]{:S(2)}, u32[]{:S(2)}) collective-permute-start(bf16[2,576,128]{2,1,0:T(8,128)(2,1)S(1)} %dynamic-slice_bitcast_fusion.2), channel_id=1, source_target_pairs={{0,16},{16,0},{1,17},{17,1},{2,18},{18,2},{3,19},{19,3},{4,20},{20... | collective-permute-start | bytes 884744 | tf_op jit(solution)/shard_map/ppermute | solution.py:337
  106.9 8.0 %collective-permute-start.7 = (bf16[576,128]{1,0:T(8,128)(2,1)S(1)}, bf16[576,128]{1,0:T(8,128)(2,1)S(1)}, u32[]{:S(2)}, u32[]{:S(2)}) collective-permute-start(bf16[576,128]{1,0:T(8,128)(2,1)S(1)} %fusion.1), channel_id=1, source_target_pairs={{32,0},{64,32},{96,64},{33,1},{65,33},{97,65},{34,2},{66,34},{98,6... | collective-permute-start | bytes 442376 | tf_op jit(solution)/shard_map/ppermute | solution.py:344
  122.1 6.6 %collective-permute-start.10 = (bf16[512,128]{1,0:T(8,128)(2,1)S(1)}, bf16[512,128]{1,0:T(8,128)(2,1)S(1)}, u32[]{:S(2)}, u32[]{:S(2)}) collective-permute-start(bf16[512,128]{1,0:T(8,128)(2,1)S(1)} %reduce_sum.32), channel_id=1, source_target_pairs={{0,64},{32,96},{64,0},{96,32},{1,65},{33,97},{65,1},{97,33},{2,66}... | collective-permute-start | bytes 393224 | tf_op jit(solution)/shard_map/ppermute | solution.py:341

commit v4 on v3

--- a/solution.py
+++ b/solution.py
@@ -339,7 +339,7 @@
     d_query = place(core_info, got, dq)
 
     across = lax.ppermute(summed(across), "x", ring(2))
-    mine = total([dw_own, from_left, from_right]).astype(BF16)
+    mine = dw_own + (from_left + from_right)
     mine = all_to_all(mine.reshape(NY * NZ, LAT, 128), ("y", "z"))
     from_next = lax.ppermute(prev_sum, "x", [(i + 1, i) for i in range(NX - 1)])
     d_latent = total([own_sum, taken[1], from_next]).astype(BF16).T

time: 130 us -> 130 us (level)
    convert_element_type x1 -> x0, other arithmetic: 5.09 us -> none  [per_device(): mine = total([dw_own, from_left, from_right]).astype(BF16)]
    add x0 -> x1, other arithmetic: none -> 4.49 us  [per_device(): mine = dw_own + (from_left + from_right)]
  transfers between devices with their start and end apart: 13 -> 13, of which waited for: 8 -> 8; matrix products, arithmetic and copies ran while one was open for 12% -> 11% of each run, Pallas kernels for 26% -> 26%
where the time goes in v4:
time: 130 us; the launch traced here: 129 us
  Pallas kernels  54.5 us (42%)
  starting transfers between devices  29.6 us (23%)
  waiting for transfers between devices  28.5 us (22%)
  other arithmetic  9.79 us (8%)
  local copies, waits for them, and re-layouts  5.83 us (4%)
    pallas_call x3, Pallas kernels, main_groups(): pl.pallas_call(functools.partial(main_kernel, groups), grid_spec=grid_spe...  44.5 us
    all_to_all x2, starting transfers between devices, all_to_all(): return lax.all_to_all(blocks, axis, 0, 0, tiled=True)  16.8 us
    ppermute x1, waiting for transfers between devices, per_device(): from_left = lax.ppermute(dw_left, 'x', ring(1))  13.9 us
    ppermute x1, waiting for transfers between devices, per_device(): from_next = lax.ppermute(prev_sum, 'x', [(i + 1, i) for i in range(NX - 1)])  6.72 us
    add x1, other arithmetic, per_device(): mine = dw_own + (from_left + from_right)  4.49 us
    pallas_call x1, Pallas kernels, fold(): pl.pallas_call(fold_kernel, grid=(KEYS // ROWS,), in_specs=[pl.BlockSpec(...  4.3 us
    unnamed x8, local copies, waits for them, and re-layouts  3.79 us
    pallas_call x1, Pallas kernels, place(): pl.pallas_call(place_kernel, grid_spec=grid_spec, out_shape=pltpu.HBM((HE...  3.56 us
  transfers between devices with their start and end apart: 13, of which 8 were waited for; matrix products, arithmetic and copies ran while one was open for 11% of the time, Pallas kernels for 26%

profile of v4, /device:TPU:8, one launch (start us, length us, event | category | flops | bytes accessed | tf_op | source)
XLA Modules:
  0.0 128.9 jit_solution(11477999910783758733)
XLA Ops:
  0.6 0.1 collective-permute-start
  0.7 3.4 %collective-permute-start.1 = (bf16[576,128]{1,0:T(8,128)(2,1)}, bf16[576,128]{1,0:T(8,128)(2,1)S(1)}, u32[]{:S(2)}, u32[]{:S(2)}) collective-permute-start(bf16[576,128]{1,0:T(8,128)(2,1)} %bitcast.82), channel_id=1, source_target_pairs={{0,32},{32,64},{64,96},{1,33},{33,65},{65,97},{2,34},{34,66},{66,9... | collective-permute-start | bytes 442376 | tf_op jit(solution)/shard_map/ppermute | solution.py:304
  4.1 0.3 collective-permute-start.2
  4.4 2.9 %copy.23 = bf16[1,128,64,128]{3,1,2,0:T(8,128)(2,1)S(1)} copy(bf16[1,128,64,128]{3,2,1,0:T(8,128)(2,1)} %param.9) | data formatting | bytes 4194304 | tf_op args[4]
  7.4 0.0 copy-start.2
  7.4 0.8 collective-permute-done.1.prev_same
  8.2 0.0 collective-permute-done.2.mate
  8.2 1.1 constant_dynamic-slice_fusion
  9.2 0.0 copy-done.1
  9.3 0.0 collective-permute-start.3
  9.3 0.0 copy-done.2
  9.3 0.2 reduce-window.8
  9.4 0.1 select_reduce_fusion
  9.5 0.5 collective-permute-start.4
  10.1 0.1 pad_add_fusion.2.info
  10.1 2.1 %collective-permute-done.4.prev_mate = bf16[576,128]{1,0:T(8,128)(2,1)} collective-permute-done((bf16[576,128]{1,0:T(8,128)(2,1)S(1)}, bf16[576,128]{1,0:T(8,128)(2,1)}, u32[]{:S(2)}, u32[]{:S(2)}) %collective-permute-start.4) | collective-permute-done | bytes 147488 | tf_op jit(solution)/shard_map/ppermute | solution.py:312
  12.3 2.2 %window.1 = (bf16[512,512]{1,0:T(8,128)(2,1)}, bf16[512,512]{1,0:T(8,128)(2,1)}, bf16[512,64]{1,0:T(8,128)(2,1)S(1)}) custom-call(s32[1]{0:T(128)} %bitcast.info, bf16[576,128]{1,0:T(8,128)(2,1)} %bitcast.84, bf16[576,128]{1,0:T(8,128)(2,1)} %copy-done.1, bf16[576,128]{1,0:T(8,128)(2,1)} %copy-done, bf16[576,128]{1,0:T(8,128)(2,1)} %collective-permute-done.4.prev_mate), custom_call_target="tpu_custom_call" | custom-call | tf_op jit(solution)/shard_map/window/pallas_call | solution.py:215
  14.4 0.0 collective-permute-done.3.refs_3_
  14.4 0.0 collective-permute-done.refs_1_
  14.4 20.8 %main_groups.3 = (bf16[64,192,128]{2,1,0:T(8,128)(2,1)}, bf16[32,192,128]{2,1,0:T(8,128)(2,1)}, bf16[4,4,512,128]{3,2,1,0:T(8,128)(2,1)}, bf16[4,4,512,128]{3,2,...) custom-call(s32[3]{0:T(128)S(1)} %pad_add_fusion.2.info, bf16[64,192,128]{2,1,0:T(8,128)(2,1)} %bitcast.73, ...), custom_call_target="tpu_custom_call" | custom-call | tf_op jit(solution)/shard_map/main_groups/pallas_call | solution.py:140
  35.2 2.4 %collective-permute-start.8 = (bf16[4,4,512,128]{3,2,1,0:T(8,128)(2,1)}, bf16[4,4,512,128]{3,2,1,0:T(8,128)(2,1)}, u32[]{:S(2)}, u32[]{:S(2)}) collective-permute-start(bf16[4,4,512,128]{3,2,1,0:T(8,128)(2,1)} %get-tuple-element.48), channel_id=1, source_target_pairs={{0,32},{32,64},{64,96},{96,0},{1,33},{33,65},{65,97},{97,1},{2,34}... | collective-permute-start | bytes 6291464 | tf_op jit(solution)/shard_map/ppermute | solution.py:325
  37.7 1.4 %collective-permute-start.9 = (bf16[4,4,512,128]{3,2,1,0:T(8,128)(2,1)}, bf16[4,4,512,128]{3,2,1,0:T(8,128)(2,1)}, u32[]{:S(2)}, u32[]{:S(2)}) collective-permute-start(bf16[4,4,512,128]{3,2,1,0:T(8,128)(2,1)} %get-tuple-element.49), channel_id=1, source_target_pairs={{0,96},{32,0},{64,32},{96,64},{1,97},{33,1},{65,33},{97,65},{2,98}... | collective-permute-start | bytes 6291464 | tf_op jit(solution)/shard_map/ppermute | solution.py:326
  39.0 0.1 pad_add_fusion
  39.1 11.8 %main_groups.4 = (bf16[64,192,128]{2,1,0:T(8,128)(2,1)}, bf16[32,192,128]{2,1,0:T(8,128)(2,1)}, bf16[4,4,512,128]{3,2,1,0:T(8,128)(2,1)}, f32[512,512]{1,0:T(8,128)}, f32[512,64]{1,0:T(8,128)}) custom-call(s32[2]{0:T(128)S(1)} %get-tuple-element.58.info, bf16[64,192,128]{2,1,0:T(8,128)(2,1)} %bitcast.74, ...), custom_call_target="tpu_custom_call", output_to_operand_aliasing={{0}: (10, {}), {1}: (11, {})} | custom-call | tf_op jit(solution)/shard_map/main_groups/pallas_call | solution.py:140
  50.9 8.4 %all-to-all-start.1 = ((bf16[16,512,128]{2,1,0:T(8,128)(2,1)}), bf16[16,512,128]{2,1,0:T(8,128)(2,1)}, u32[]{:S(2)}, u32[]{:S(2)}) async-start(bf16[16,512,128]{2,1,0:T(8,128)(2,1)} %bitcast.78), calls=%async_computation.1 | async-start | bytes 4194304 | tf_op jit(solution)/shard_map/all_to_all | solution.py:284
  59.4 11.9 %main_groups.5 = (bf16[64,192,128]{2,1,0:T(8,128)(2,1)}, bf16[32,192,128]{2,1,0:T(8,128)(2,1)}, bf16[4,4,512,128]{3,2,1,0:T(8,128)(2,1)}, f32[512,512]{1,0:T(8,128)}, f32[512,64]{1,0:T(8,128)}) custom-call(s32[2]{0:T(128)S(1)} %get-tuple-element.57.info, bf16[64,192,128]{2,1,0:T(8,128)(2,1)} %bitcast.75, ...), custom_call_target="tpu_custom_call", output_to_operand_aliasing={{0}: (10, {}), {1}: (11, {})} | custom-call | tf_op jit(solution)/shard_map/main_groups/pallas_call | solution.py:140
  71.2 13.9 %collective-permute-done.8 = bf16[4,4,512,128]{3,2,1,0:T(8,128)(2,1)} collective-permute-done((bf16[4,4,512,128]{3,2,1,0:T(8,128)(2,1)}, bf16[4,4,512,128]{3,2,1,0:T(8,128)(2,1)}, u32[]{:S(2)}, u32[]{:S(2)}) %collective-permute-start.8) | collective-permute-done | bytes 2097184 | tf_op jit(solution)/shard_map/ppermute | solution.py:325
  85.2 0.2 collective-permute-done.9
  85.4 4.5 %add_add_fusion = bf16[4,4,512,128]{3,2,1,0:T(8,128)(2,1)} fusion(bf16[4,4,512,128]{3,2,1,0:T(8,128)(2,1)} %get-tuple-element.47, bf16[4,4,512,128]{3,2,1,0:T(8,128)(2,1)} %collective-permute-done.8, bf16[4,4,512,128]{3,2,1,0:T(8,128)(2,1)} %collective-permute-done.9), kind=kLoop, calls=%fused_computation.2 | loop fusion | flops 2097152 | bytes 8388608 | tf_op jit(solution)/shard_map/add | solution.py:342
  89.9 0.0 all-to-all-done.1
  89.9 8.4 %all-to-all-start = ((bf16[16,512,128]{2,1,0:T(8,128)(2,1)}), bf16[16,512,128]{2,1,0:T(8,128)(2,1)S(1)}, u32[]{:S(2)}, u32[]{:S(2)}) async-start(bf16[16,512,128]{2,1,0:T(8,128)(2,1)} %bitcast.77), calls=%async_computation | async-start | bytes 4194304 | tf_op jit(solution)/shard_map/all_to_all | solution.py:284
  98.3 0.0 collective-permute-start.5
  98.3 4.3 %fold.1 = (f32[4,576,128]{2,1,0:T(8,128)}, bf16[4,576,128]{2,1,0:T(8,128)(2,1)}) custom-call(f32[512,512]{1,0:T(8,128)} %get-tuple-element.39.refs_0_, f32[512,64]{1,0:T(8,128)} %get-tuple-element.40.refs_1_, f32[512,512]{1,0:T(8,128)} %get-tuple-element.41.refs_2_, f32[512,64]{1,0:T(8,128)} %get-tuple-element.42.refs_3_, ...), custom_call_target="tpu_custom_call" | custom-call | tf_op jit(solution)/shard_map/fold/pallas_call | solution.py:174
  102.6 1.0 dynamic-slice_bitcast_fusion.2
  103.6 0.6 collective-permute-start.6
  104.1 1.2 collective-permute-done.6
  105.3 1.0 fusion.1
  106.3 1.3 %collective-permute-start.7 = (bf16[576,128]{1,0:T(8,128)(2,1)S(1)}, bf16[576,128]{1,0:T(8,128)(2,1)S(1)}, u32[]{:S(2)}, u32[]{:S(2)}) collective-permute-start(bf16[576,128]{1,0:T(8,128)(2,1)S(1)} %fusion.1), channel_id=1, source_target_pairs={{32,0},{64,32},{96,64},{33,1},{65,33},{97,65},{34,2},{66,34},{98,6... | collective-permute-start | bytes 442376 | tf_op jit(solution)/shard_map/ppermute | solution.py:344
  107.6 6.7 %collective-permute-done.7 = bf16[576,128]{1,0:T(8,128)(2,1)S(1)} collective-permute-done((bf16[576,128]{1,0:T(8,128)(2,1)S(1)}, bf16[576,128]{1,0:T(8,128)(2,1)S(1)}, u32[]{:S(2)}, u32[]{:S(2)}) %collective-permute-start.7) | collective-permute-done | bytes 147488 | tf_op jit(solution)/shard_map/ppermute | solution.py:344
  114.4 1.7 %fusion.5 = bf16[1,128,576]{1,2,0:T(8,128)(2,1)} fusion(bf16[576,128]{1,0:T(8,128)(2,1)S(1)} %collective-permute-done.7, f32[2,2,576,128]{3,2,1,0:T(8,128)} %bitcast.80, s32[]{:T(128)S(6)} %add.66, s32[]{:T(128)S(6)} %select_n.16, bf16[2,576,128]{2,1,0:T(8,128)(2,1)S(1)} %collective-permute-done.6), kind=kLoop, calls=%fused_computation.12 | loop fusion | flops 368640 | bytes 737288 | tf_op jit(solution)/shard_map/broadcast_in_dim | solution.py:348
  116.0 0.0 collective-permute-done.5.got_ref
  116.0 3.6 %place.1 = bf16[64,192,128]{2,1,0:T(8,128)(2,1)} custom-call(s32[1]{0:T(128)} %bitcast.info, bf16[32,192,128]{2,1,0:T(8,128)(2,1)} %collective-permute-done.5.got_ref, bf16[64,192,128]{2,1,0:T(8,128)(2,1)} %get-tuple-element.38.held_ref), custom_call_target="tpu_custom_call", output_to_operand_aliasing={{}: (2, {})} | custom-call | tf_op jit(solution)/shard_map/place/pallas_call | solution.py:246
  119.6 1.9 %reduce_sum.32 = bf16[512,128]{1,0:T(8,128)(2,1)S(1)} reduce(bf16[16,512,128]{2,1,0:T(8,128)(2,1)} %all-to-all-done.1, bf16[]{:T(256)} %constant.52.clone.1), dimensions={0}, to_apply=%region_3.4 | reduce | flops 983040 | bytes 2228226 | tf_op jit(solution)/shard_map/reduce_sum | solution.py:288
  121.5 2.8 %collective-permute-start.10 = (bf16[512,128]{1,0:T(8,128)(2,1)S(1)}, bf16[512,128]{1,0:T(8,128)(2,1)S(1)}, u32[]{:S(2)}, u32[]{:S(2)}) collective-permute-start(bf16[512,128]{1,0:T(8,128)(2,1)S(1)} %reduce_sum.32), channel_id=1, source_target_pairs={{0,64},{32,96},{64,0},{96,32},{1,65},{33,97},{65,1},{97,33},{2,66}... | collective-permute-start | bytes 393224 | tf_op jit(solution)/shard_map/ppermute | solution.py:341
  124.3 0.7 all-to-all-done
  125.0 0.3 convert_reduce_fusion
  125.3 2.7 %collective-permute-done.10 = bf16[512,128]{1,0:T(8,128)(2,1)S(1)} collective-permute-done((bf16[512,128]{1,0:T(8,128)(2,1)S(1)}, bf16[512,128]{1,0:T(8,128)(2,1)S(1)}, u32[]{:S(2)}, u32[]{:S(2)}) %collective-permute-start.10) | collective-permute-done | bytes 131104 | tf_op jit(solution)/shard_map/ppermute | solution.py:341
  128.1 0.8 copy.20
  (6 shorter events, 0.0 us)
Async XLA Ops:
  0.6 13.8 %collective-permute-start = (bf16[64,192,128]{2,1,0:T(8,128)(2,1)}, bf16[64,192,128]{2,1,0:T(8,128)(2,1)}, u32[]{:S(2)}, u32[]{:S(2)}) collective-permute-start(bf16[64,192,128]{2,1,0:T(8,128)(2,1)} %bitcast.72), channel_id=1, source_target_pairs={{0,16},{16,0},{1,17},{17,1},{2,18},{18,2},{3,19},{19,3},{4,20},{20... | collective-permute-start | bytes 9437192 | tf_op jit(solution)/shard_map/ppermute | solution.py:306
  0.7 7.5 %collective-permute-start.1 = (bf16[576,128]{1,0:T(8,128)(2,1)}, bf16[576,128]{1,0:T(8,128)(2,1)S(1)}, u32[]{:S(2)}, u32[]{:S(2)}) collective-permute-start(bf16[576,128]{1,0:T(8,128)(2,1)} %bitcast.82), channel_id=1, source_target_pairs={{0,32},{32,64},{64,96},{1,33},{33,65},{65,97},{2,34},{34,66},{66,9... | collective-permute-start | bytes 442376 | tf_op jit(solution)/shard_map/ppermute | solution.py:304
  4.1 4.0 %collective-permute-start.2 = (bf16[576,128]{1,0:T(8,128)(2,1)}, bf16[576,128]{1,0:T(8,128)(2,1)S(1)}, u32[]{:S(2)}, u32[]{:S(2)}) collective-permute-start(bf16[576,128]{1,0:T(8,128)(2,1)} %bitcast.83), channel_id=1, source_target_pairs={{0,16},{16,0},{1,17},{17,1},{2,18},{18,2},{3,19},{19,3},{4,20},{20... | collective-permute-start | bytes 442376 | tf_op jit(solution)/shard_map/ppermute | solution.py:303
  7.4 1.9 %copy-start.2 = (s32[1,8]{1,0:T(1,128)S(1)}, s32[1,8]{1,0:T(1,128)}, u32[]{:S(2)}) copy-start(s32[1,8]{1,0:T(1,128)} %param.7) | copy-start | bytes 100
  8.2 4.1 %copy-start = (bf16[576,128]{1,0:T(8,128)(2,1)}, bf16[576,128]{1,0:T(8,128)(2,1)S(1)}, u32[]{:S(2)}) copy-start(bf16[576,128]{1,0:T(8,128)(2,1)S(1)} %collective-permute-done.1.prev_same) | copy-start | bytes 442372
  8.2 1.1 copy-start.1
  9.3 5.2 %collective-permute-start.3 = (bf16[32,128,128]{2,1,0:T(8,128)(2,1)}, bf16[32,128,128]{2,1,0:T(8,128)(2,1)S(1)}, u32[]{:S(2)}, u32[]{:S(2)}) collective-permute-start(bf16[32,128,128]{2,1,0:T(8,128)(2,1)} %bitcast.11), channel_id=1, source_target_pairs={{0,16},{16,0},{1,17},{17,1},{2,18},{18,2},{3,19},{19,3},{4,20},{20... | collective-permute-start | bytes 3145736 | tf_op jit(solution)/shard_map/ppermute | solution.py:309
  9.5 2.7 %collective-permute-start.4 = (bf16[576,128]{1,0:T(8,128)(2,1)S(1)}, bf16[576,128]{1,0:T(8,128)(2,1)}, u32[]{:S(2)}, u32[]{:S(2)}) collective-permute-start(bf16[576,128]{1,0:T(8,128)(2,1)S(1)} %collective-permute-done.1.prev_same), channel_id=1, source_target_pairs={{0,16},{16,0},{1,17},{17,1},{2,18},{18,2},{3,19},{19,3},{4,20},{20... | collective-permute-start | bytes 442376 | tf_op jit(solution)/shard_map/ppermute | solution.py:312
  35.2 50.0 %collective-permute-start.8 = (bf16[4,4,512,128]{3,2,1,0:T(8,128)(2,1)}, bf16[4,4,512,128]{3,2,1,0:T(8,128)(2,1)}, u32[]{:S(2)}, u32[]{:S(2)}) collective-permute-start(bf16[4,4,512,128]{3,2,1,0:T(8,128)(2,1)} %get-tuple-element.48), channel_id=1, source_target_pairs={{0,32},{32,64},{64,96},{96,0},{1,33},{33,65},{65,97},{97,1},{2,34}... | collective-permute-start | bytes 6291464 | tf_op jit(solution)/shard_map/ppermute | solution.py:325
  37.7 47.7 %collective-permute-start.9 = (bf16[4,4,512,128]{3,2,1,0:T(8,128)(2,1)}, bf16[4,4,512,128]{3,2,1,0:T(8,128)(2,1)}, u32[]{:S(2)}, u32[]{:S(2)}) collective-permute-start(bf16[4,4,512,128]{3,2,1,0:T(8,128)(2,1)} %get-tuple-element.49), channel_id=1, source_target_pairs={{0,96},{32,0},{64,32},{96,64},{1,97},{33,1},{65,33},{97,65},{2,98}... | collective-permute-start | bytes 6291464 | tf_op jit(solution)/shard_map/ppermute | solution.py:326
  50.9 38.9 %all-to-all-start.1 = ((bf16[16,512,128]{2,1,0:T(8,128)(2,1)}), bf16[16,512,128]{2,1,0:T(8,128)(2,1)}, u32[]{:S(2)}, u32[]{:S(2)}) async-start(bf16[16,512,128]{2,1,0:T(8,128)(2,1)} %bitcast.78), calls=%async_computation.1 | async-start | bytes 4194304 | tf_op jit(solution)/shard_map/all_to_all | solution.py:284
  89.9 35.2 %all-to-all-start = ((bf16[16,512,128]{2,1,0:T(8,128)(2,1)}), bf16[16,512,128]{2,1,0:T(8,128)(2,1)S(1)}, u32[]{:S(2)}, u32[]{:S(2)}) async-start(bf16[16,512,128]{2,1,0:T(8,128)(2,1)} %bitcast.77), calls=%async_computation | async-start | bytes 4194304 | tf_op jit(solution)/shard_map/all_to_all | solution.py:284
  98.3 17.8 %collective-permute-start.5 = (bf16[32,192,128]{2,1,0:T(8,128)(2,1)}, bf16[32,192,128]{2,1,0:T(8,128)(2,1)}, u32[]{:S(2)}, u32[]{:S(2)}) collective-permute-start(bf16[32,192,128]{2,1,0:T(8,128)(2,1)} %get-tuple-element.37), channel_id=1, source_target_pairs={{0,16},{16,0},{1,17},{17,1},{2,18},{18,2},{3,19},{19,3},{4,20},{20... | collective-permute-start | bytes 4718600 | tf_op jit(solution)/shard_map/ppermute | solution.py:331
  103.6 1.8 %collective-permute-start.6 = (bf16[2,576,128]{2,1,0:T(8,128)(2,1)S(1)}, bf16[2,576,128]{2,1,0:T(8,128)(2,1)S(1)}, u32[]{:S(2)}, u32[]{:S(2)}) collective-permute-start(bf16[2,576,128]{2,1,0:T(8,128)(2,1)S(1)} %dynamic-slice_bitcast_fusion.2), channel_id=1, source_target_pairs={{0,16},{16,0},{1,17},{17,1},{2,18},{18,2},{3,19},{19,3},{4,20},{20... | collective-permute-start | bytes 884744 | tf_op jit(solution)/shard_map/ppermute | solution.py:337
  106.3 8.0 %collective-permute-start.7 = (bf16[576,128]{1,0:T(8,128)(2,1)S(1)}, bf16[576,128]{1,0:T(8,128)(2,1)S(1)}, u32[]{:S(2)}, u32[]{:S(2)}) collective-permute-start(bf16[576,128]{1,0:T(8,128)(2,1)S(1)} %fusion.1), channel_id=1, source_target_pairs={{32,0},{64,32},{96,64},{33,1},{65,33},{97,65},{34,2},{66,34},{98,6... | collective-permute-start | bytes 442376 | tf_op jit(solution)/shard_map/ppermute | solution.py:344
  121.5 6.6 %collective-permute-start.10 = (bf16[512,128]{1,0:T(8,128)(2,1)S(1)}, bf16[512,128]{1,0:T(8,128)(2,1)S(1)}, u32[]{:S(2)}, u32[]{:S(2)}) collective-permute-start(bf16[512,128]{1,0:T(8,128)(2,1)S(1)} %reduce_sum.32), channel_id=1, source_target_pairs={{0,64},{32,96},{64,0},{96,32},{1,65},{33,97},{65,1},{97,33},{2,66}... | collective-permute-start | bytes 393224 | tf_op jit(solution)/shard_map/ppermute | solution.py:341
